TPU v7x, 128 devices: a whole 4x4x4 slice. The times are simulated.
128 devices in a mesh: blk: 32 (over x_lo, y, z), corpus: 4 (over x_hi, core).
Axes of the slice: x: 4 (x_hi: 2, x_lo: 2; x = x_hi * 2 + x_lo), y: 4, z: 4, core: 2. Of those that a mesh axis runs over, the one named last changes fastest.
Arguments:
- queries: bfloat16 [4096, 4096], P('blk', 'corpus'), may hold values from -12 to 12
- passages: bfloat16 [4096, 4096], P('blk', 'corpus'), may hold values from -4 to 4
- table: bfloat16 [1024, 4096], P('corpus'), may hold values from -4 to 4
- neg_owner: int32 [4096, 7], P('blk'), may hold values from 0 to 3, as said below
- neg_row: int32 [4096, 7], P('blk'), may hold values from 0 to 255
- positive: int32 [4096], P('blk'), may hold values from 0 to 4095, each once
- loss_weight: float32 [4096], P('blk'), may hold values from 32 to 256
Outputs:
- losses: float32 [4096], P(('blk', 'corpus'))
- query_grad: float32 [4096, 4096], P('blk', 'corpus')
- passage_grad: float32 [4096, 4096], P('blk', 'corpus')
- table_grad: float32 [1024, 4096], P('corpus', 'blk')
Inputs may be any that keep to these rules, and one draw needn't show every extreme that they name: `neg_owner`: among the 896 references of the queries of one index of blk (aligned blocks of 128 queries), one shard is named exactly 448 times and no shard more often.
All inputs are finite; a program needn't handle non-finite values.
Results may differ from a plain program's by a relative error of at most 0.0065.
Values may be sent and summed in bfloat16 or wider, within the bound.
A program may use at most 128 MiB of HBM per device.

v0:
```python
import jax
import jax.numpy as jnp
from jax import lax
from jax.sharding import PartitionSpec as P

CAP = 448


def split_product(mixing, right_side):
    upper = mixing.astype(jnp.bfloat16)
    lower = (mixing - upper.astype(jnp.float32)).astype(jnp.bfloat16)
    return jnp.dot(upper, right_side, preferred_element_type=jnp.float32) + jnp.dot(
        lower, right_side, preferred_element_type=jnp.float32
    )


def per_device(queries, passages, table, neg_owner, neg_row, positive, loss_weight):
    q_rows, col_width = queries.shape
    owner_count = lax.axis_size("corpus")
    factor = (col_width * owner_count) ** (-0.5)
    rows_shard = table.shape[0]
    negs = neg_owner.shape[1]
    ref_count = q_rows * negs
    owners = neg_owner.reshape(ref_count)
    neg_rows = neg_row.reshape(ref_count)
    owner_index = lax.axis_index("corpus")
    all_passages = lax.all_gather(passages, "blk", axis=0, tiled=True)
    all_rows = all_passages.shape[0]
    owner_marks = (owners[:, None] == jnp.arange(owner_count, dtype=jnp.int32)[None, :]).astype(
        jnp.int32
    )
    slot_ranks = jnp.sum(jnp.cumsum(owner_marks, axis=0) * owner_marks, axis=1) - 1
    slot_index = owners * CAP + slot_ranks
    target = jnp.where(owners == owner_index, slot_ranks, CAP)
    wanted = jnp.zeros((CAP,), jnp.int32).at[target].set(neg_rows, mode="drop")
    outgoing = table[wanted]
    arrived = lax.all_to_all(outgoing, "corpus", split_axis=1, concat_axis=0, tiled=True)
    picked = arrived[slot_index]
    hard_rows = picked.reshape(q_rows, negs, col_width)
    logits = lax.dot_general(
        queries, all_passages, (((1,), (1,)), ((), ())), preferred_element_type=jnp.float32
    )
    hard_logits = jnp.einsum("qd,qkd->qk", queries, hard_rows, preferred_element_type=jnp.float32)
    logits, hard_logits = lax.psum((logits, hard_logits), "corpus")
    logits = logits * factor
    hard_logits = hard_logits * factor
    row_top = jnp.maximum(jnp.max(logits, axis=1), jnp.max(hard_logits, axis=1))
    log_total = row_top + jnp.log(
        jnp.sum(jnp.exp(logits - row_top[:, None]), axis=1)
        + jnp.sum(jnp.exp(hard_logits - row_top[:, None]), axis=1)
    )
    one_hot = positive[:, None] == jnp.arange(all_rows, dtype=jnp.int32)[None, :]
    losses = log_total - jnp.sum(jnp.where(one_hot, logits, 0.0), axis=1)
    share = q_rows // owner_count
    loss_share = lax.dynamic_slice_in_dim(losses, owner_index * share, share)
    weighting = (loss_weight * factor)[:, None]
    soft_grad = (
        weighting * (jnp.exp(logits - log_total[:, None]) - one_hot.astype(jnp.float32))
    ).astype(jnp.bfloat16)
    hard_grad = (weighting * jnp.exp(hard_logits - log_total[:, None])).astype(jnp.bfloat16)
    query_grad = jnp.dot(soft_grad, all_passages, preferred_element_type=jnp.float32)
    query_grad = query_grad + jnp.einsum(
        "qk,qkd->qd", hard_grad, hard_rows, preferred_element_type=jnp.float32
    )
    passage_grad = lax.psum_scatter(
        lax.dot_general(
            soft_grad, queries, (((0,), (0,)), ((), ())), preferred_element_type=jnp.float32
        ),
        "blk",
        scatter_dimension=0,
        tiled=True,
    )
    table_rows = owner_count * rows_shard
    flat_ids = owners * rows_shard + neg_rows
    query_of = jnp.arange(ref_count, dtype=jnp.int32) // negs
    mixing = (
        jnp.zeros((table_rows, q_rows), jnp.float32)
        .at[flat_ids, query_of]
        .add(hard_grad.reshape(ref_count).astype(jnp.float32))
    )
    dense_grad = split_product(mixing, queries)
    owned_grad = lax.all_to_all(dense_grad, "corpus", split_axis=0, concat_axis=1, tiled=True)
    table_grad = lax.psum_scatter(owned_grad, "blk", scatter_dimension=1, tiled=True)
    return (loss_share, query_grad, passage_grad, table_grad)


def solution(mesh):
    placed = (
        P("blk", "corpus"),
        P("blk", "corpus"),
        P("corpus", None),
        P("blk", None),
        P("blk", None),
        P("blk"),
        P("blk"),
    )
    return jax.shard_map(
        per_device,
        mesh=mesh,
        in_specs=placed,
        out_specs=(
            P(("blk", "corpus")),
            P("blk", "corpus"),
            P("blk", "corpus"),
            P("corpus", "blk"),
        ),
        check_vma=False,
    )
```

profile of v0, /device:TPU:0, one launch (start us, length us, event | category | flops | bytes accessed | tf_op | source)
XLA Modules:
  0.0 738.2 jit_solution(4839107466611994466)
XLA Ops:
  7.2 0.0 copy-start
  7.2 0.0 all-gather.2.cloned.1.call-start
  7.2 0.7 all-gather.2.cloned.1.call-update
  7.9 0.8 copy.30
  8.7 0.2 eq.61
  8.9 0.2 eq.57
  9.1 0.8 copy.32
  9.9 0.7 multiply_add_fusion
  10.6 0.1 copy.34
  10.7 0.2 mul.71
  11.0 1.1 reduce-window.6
  12.1 0.2 slice_reduce_fusion
  12.3 0.2 reduce-window.9
  12.5 0.7 broadcast_compare_fusion
  13.2 0.1 copy.29
  13.3 0.2 eq.56
  13.6 0.2 reshape.219
  13.8 0.1 add_bitcast_fusion
  13.9 5.3 scatter_custom_fusion
  19.2 0.0 copy-done
  19.2 4.2 gather_fusion
  23.4 4.4 copy.50
  27.8 0.0 copy-start.3
  27.8 4.9 all-to-all-start
  32.7 0.0 all-reduce.2.cloned.1.call-start
  32.8 157.7 %all-gather.2.cloned.1.call-done = bf16[4096,1024]{1,0:T(8,128)(2,1)} async-done(((bf16[128,1024]{1,0:T(8,128)(2,1)}), bf16[4096,1024]{1,0:T(8,128)(2,1)}) %all-gather.2.cloned.1.call-update) | async-done | bytes 8388624 | tf_op jit(solution)/shard_map/all_gather | solution.py:27
  190.4 0.0 copy-done.3
  190.4 7.6 %fusion.18 = f32[128,4096]{1,0:T(8,128)} fusion(bf16[128,1024]{1,0:T(8,128)(2,1)S(1)} %copy-done.3, bf16[4096,1024]{1,0:T(8,128)(2,1)} %all-gather.2.cloned.1.call-done), kind=kOutput, calls=%fused_computation.59 | convolution fusion | flops 1073741824 | bytes 10747904 | tf_op jit(solution)/shard_map/dot_general | solution.py:40
  198.1 0.0 copy-start.5
  198.1 0.0 all-reduce.2.cloned.1.call-update
  198.1 0.0 reduce-scatter.5.cloned.1.call-start
  198.2 0.1 copy.35
  198.3 0.2 add.143
  198.5 0.2 copy-done.5
  198.7 0.0 all-to-all-done
  198.7 8.0 %gather_fusion.1 = bf16[896,1024]{1,0:T(8,128)(2,1)} fusion(bf16[1792,1024]{1,0:T(8,128)(2,1)} %bitcast.2, s32[1024]{0:T(1024)S(1)} %pad_clamp_fusion), kind=kCustom, calls=%fused_computation.1 | custom fusion | bytes 3673600 | tf_op jit(solution)/shard_map/gather | solution.py:38
  206.8 3.9 reshape.197
  210.7 2.9 fusion
  213.5 0.0 copy-start.4
  213.6 0.1 copy.39
  213.6 7.8 %psum.15 = f32[128,7]{0,1:T(8,128)S(1)} all-reduce(f32[128,7]{0,1:T(8,128)S(1)} %bitcast.47), channel_id=1, replica_groups=mesh['blk'=32,'corpus'=4] {'corpus'}, use_global_device_ids=true, to_apply=%region_6.7 | all-reduce | flops 896 | bytes 7168 | tf_op jit(solution)/shard_map/psum | solution.py:44
  221.5 35.9 %all-reduce.2.cloned.1.call-done = f32[128,4096]{1,0:T(8,128)} async-done(((f32[128,4096]{1,0:T(8,128)}), f32[128,4096]{1,0:T(8,128)}) %all-reduce.2.cloned.1.call-update) | async-done | bytes 2097168 | tf_op jit(solution)/shard_map/psum | solution.py:44
  257.3 2.0 multiply_reduce_fusion
  259.3 0.0 copy-done.4
  259.3 0.2 copy-done.1
  259.6 0.8 select_reduce_fusion
  260.4 0.1 copy.36
  260.5 0.2 reshape.225
  260.7 44.6 %scatter_fusion = f32[1024,128]{1,0:T(8,128)S(1)} fusion(f32[1024,128]{1,0:T(8,128)S(1)} %broadcast_in_dim.32, s32[896]{0:T(1024)S(1)} %fusion.11, f32[896]{0:T(1024)S(1)} %reshape.225), kind=kCustom, calls=%fused_computation.3 | custom fusion | flops 896 | bytes 17920 | tf_op jit(solution)/shard_map/scatter-add | solution.py:79
  305.3 0.7 fusion.3
  306.0 0.7 convolution_add_fusion
  306.7 52.2 %all_to_all.38 = f32[4,256,1024]{2,1,0:T(8,128)S(1)} all-to-all(f32[4,256,1024]{2,1,0:T(8,128)S(1)} %bitcast.42), channel_id=1, replica_groups=mesh['blk'=32,'corpus'=4] {'corpus'}, dimensions={0} | all-to-all | bytes 8388608 | tf_op jit(solution)/shard_map/all_to_all | solution.py:82
  359.0 2.3 copy.43
  361.2 0.0 reduce-scatter.5.cloned.1.call-update
  361.3 0.0 reduce-scatter.3.cloned.1.call-start
  361.3 9.9 %fusion.16 = f32[4096,1024]{1,0:T(8,128)} fusion(bf16[128,1024]{1,0:T(8,128)(2,1)S(1)} %copy-done.3, f32[128,4096]{1,0:T(8,128)} %all-reduce.2.cloned.1.call-done, f32[128]{0:T(128)S(1)} %get-tuple-element.9, f32[128]{0:T(128)S(1)} %broadcast_multiply_fusion.1, s32[128]{0:T(128)S(1)} %copy-done.4), kind=kOutput, calls=%fused_computation.57 | convolution fusion | flops 1077411840 | bytes 19138048 | tf_op jit(solution)/shard_map/dot_general | solution.py:66
  371.2 0.0 reduce-scatter.3.cloned.1.call-update
  371.3 0.1 copy.40
  371.4 0.6 dynamic_slice.3
  372.0 2.3 fusion.19
  374.3 0.0 copy-done.2
  374.3 5.9 convolution_add_fusion.1
  380.3 148.2 %reduce-scatter.5.cloned.1.call-done = f32[256,128]{1,0:T(8,128)} async-done(((f32[256,4096]{1,0:T(8,128)}), f32[256,128]{1,0:T(8,128)}) %reduce-scatter.5.cloned.1.call-update) | async-done | bytes 131088 | tf_op jit(solution)/shard_map/reduce_scatter | solution.py:83
  528.5 203.3 %reduce-scatter.3.cloned.1.call-done = f32[128,1024]{1,0:T(8,128)} async-done(((f32[4096,1024]{1,0:T(8,128)}), f32[128,1024]{1,0:T(8,128)}) %reduce-scatter.3.cloned.1.call-update) | async-done | bytes 524304 | tf_op jit(solution)/shard_map/reduce_scatter | solution.py:65
  (17 shorter events, 0.2 us)
Async XLA Ops:
  7.2 12.1 %copy-start = (bf16[256,4096]{1,0:T(8,128)(2,1)S(1)}, bf16[256,4096]{1,0:T(8,128)(2,1)}, u32[]{:S(2)}) copy-start(bf16[256,4096]{1,0:T(8,128)(2,1)} %param.9) | copy-start | bytes 6291460
  7.2 183.2 %all-gather.2.cloned.1.call-start = ((), (), s32[]{:S(2)}) async-start(), calls=%async_computation.4 | async-start | bytes 8650752 | tf_op jit(solution)/shard_map/all_gather | solution.py:27
  27.8 162.6 %copy-start.3 = (bf16[128,1024]{1,0:T(8,128)(2,1)S(1)}, bf16[128,1024]{1,0:T(8,128)(2,1)}, u32[]{:S(2)}) copy-start(bf16[128,1024]{1,0:T(8,128)(2,1)} %param.7) | copy-start | bytes 786436
  27.8 170.9 %all-to-all-start = ((bf16[448,4,1024]{2,0,1:T(8,128)(2,1)}), bf16[448,4,1024]{2,0,1:T(8,128)(2,1)}, u32[]{:S(2)}, u32[]{:S(2)}) async-start(bf16[448,4,1024]{2,0,1:T(8,128)(2,1)} %bitcast.45), calls=%async_computation | async-start | bytes 7340032 | tf_op jit(solution)/shard_map/all_to_all | solution.py:37
  32.7 224.6 %all-reduce.2.cloned.1.call-start = ((), (), s32[]{:S(2)}) async-start(), calls=%async_computation.5 | async-start | bytes 4194304 | tf_op jit(solution)/shard_map/psum | solution.py:44
  198.1 0.7 copy-start.5
  198.1 330.3 %reduce-scatter.5.cloned.1.call-start = ((), (), s32[]{:S(2)}) async-start(), calls=%async_computation.7 | async-start | bytes 4325376 | tf_op jit(solution)/shard_map/reduce_scatter | solution.py:83
  213.5 45.8 %copy-start.4 = (s32[128]{0:T(128)S(1)}, s32[128]{0:T(128)}, u32[]{:S(2)}) copy-start(s32[128]{0:T(128)} %param.12) | copy-start | bytes 1540
  257.3 2.2 copy-start.1
  361.3 370.5 %reduce-scatter.3.cloned.1.call-start = ((), (), s32[]{:S(2)}) async-start(), calls=%async_computation.6 | async-start | bytes 17301504 | tf_op jit(solution)/shard_map/reduce_scatter | solution.py:65
  371.4 2.9 copy-start.2
Sparse Core Ops, SparseCore 0:
  9.7 180.7 all-gather.1
  198.2 59.0 all-reduce.1
  361.4 167.0 reduce-scatter.4
  531.4 200.2 reduce-scatter.2
where the time goes:
time: 739 us; the launch traced here: 738 us
  waiting for transfers between devices  546 us (74%)
  blocking collectives  60.1 us (8%)
  other arithmetic  50.3 us (7%)
  local copies, waits for them, and re-layouts  33.1 us (4%)
  matrix products  30.1 us (4%)
  between operations  14 us (2%)
    reduce_scatter x1, waiting for transfers between devices, per_device(): lax.psum_scatter(lax.dot_general(soft_grad, queries, (((0,), (0,)), ((),...  203 us
    all_gather x1, waiting for transfers between devices, per_device(): all_passages = lax.all_gather(passages, 'blk', axis=0, tiled=True)  158 us
    reduce_scatter x1, waiting for transfers between devices, per_device(): lax.psum_scatter(owned_grad, 'blk', scatter_dimension=1, tiled=True)  148 us
    all_to_all x1, blocking collectives, per_device(): lax.all_to_all(dense_grad, 'corpus', split_axis=0, concat_axis=1, tiled=T...  52.2 us
    scatter-add x1, other arithmetic, per_device(): mixing = jnp.zeros((table_rows, q_rows), jnp.float32).at[flat_ids, query_...  44.6 us
    psum x1, waiting for transfers between devices, per_device(): logits, hard_logits = lax.psum((logits, hard_logits), 'corpus')  35.9 us
  transfers between devices with their start and end apart: 5, of which 4 were waited for; matrix products, arithmetic and copies ran while one was open for 8% of the time, Pallas kernels for 0%

commit v1 on v0

v1 whole, which is shorter than its diff:
```python
import functools

import jax
import jax.numpy as jnp
from jax import lax
from jax.experimental import pallas as pl
from jax.experimental.pallas import tpu as pltpu
from jax.sharding import PartitionSpec as P

MESH = pl.DeviceIdType.MESH
F32 = jnp.float32
BF16 = jnp.bfloat16

R = 128
W = 1024
NB = 4
TR = 64
COLS = NB * R + 2 * TR
CW = 256


def device(x, y, z, k):
    return (lax.rem(x, 2) * 16 + y * 4 + z, lax.div(x, 2) * 2 + k)


def kernel(
    factor, q_in, p_in, t_in, idx_in, loss_out, qg_out, pg_out, tg_out,
    qb, pt, idx, s_own, s_far, e_buf, grad, stats, qg_part, pg_part, tg_part,
    rq, rqx, rp, rpx, rt, tt, qx, px, tsum,
    q_s, q_r, p_s, p_r, t_s, i_s, i_r, c_s, c_r, st_s, st_r,
    qg_s, qg_r, qx_s, pg_s, pg_r, px_s, px_r, tg_s, tg_r, tt_s, tt_r,
):
    b, c = lax.axis_index("blk"), lax.axis_index("corpus")
    xl, y, z = lax.div(b, 16), lax.rem(lax.div(b, 4), 4), lax.rem(b, 4)
    xh, k = lax.div(c, 2), lax.rem(c, 2)
    x = 2 * xh + xl
    far = 1 - xh
    opposite = lax.rem(x + 2, 4)
    sibling = device(x, y, z, 1 - k)

    def send(src, dst, ss, rs, where):
        copy = pltpu.make_async_remote_copy(
            src_ref=src, dst_ref=dst, send_sem=ss, recv_sem=rs, device_id=where, device_id_type=MESH
        )
        copy.start()
        return copy

    def arrive(dst, rs):
        pltpu.make_async_remote_copy(
            src_ref=dst, dst_ref=dst, send_sem=rs, recv_sem=rs, device_id=sibling, device_id_type=MESH
        ).wait_recv()

    def turn(v, d):
        return lax.rem(v + d, 4)

    barrier = pltpu.get_barrier_semaphore()
    peers = [sibling]
    for d in (1, 2, 3):
        peers.append(device(x, y, turn(z, d), k))
        peers.append(device(x, turn(y, d), z, k))
        peers.append(device(turn(x, d), y, z, k))
        peers.append(device(opposite, y, turn(z, d), k))
        peers.append(device(2 * xh + (1 - xl), turn(y, d), z, k))
    for peer in peers:
        pl.semaphore_signal(barrier, 1, device_id=peer, device_id_type=MESH)
    src_y = 2 * lax.rem(y, 2) + lax.div(z, 2)
    src_k = lax.div(y, 2)
    for zz in range(4):
        pl.semaphore_signal(barrier, 1, device_id=device(x, src_y, zz, src_k), device_id_type=MESH)
    pl.semaphore_wait(barrier, len(peers) + 4)

    def rows(i, n=R):
        return pl.ds(pl.multiple_of(i * n, n), n)

    sends = []
    for t in range(2):
        @pl.when(x != 2 * xl + t)
        def _():
            send(p_in, pt.at[xh, rows(y)], p_s.at[t], p_r.at[xh, y], device(2 * xl + t, y, z, k))
    sends.append(send(q_in, qb.at[xh, rows(z)], q_s.at[0, 0], q_r.at[xh, z], device(opposite, y, z, k)))
    for d in (1, 2, 3):
        to = device(x, y, turn(z, d), k)
        sends.append(send(idx_in, idx.at[:, rows(z)], i_s.at[d], i_r.at[z], to))
        sends.append(send(q_in, qb.at[xh, rows(z)], q_s.at[0, d], q_r.at[xh, z], to))
    table_rows = pl.ds(NB * R + pl.multiple_of(k * TR, TR), TR)
    local = []
    for s in range(2):
        def part(core):
            return t_in.at[rows(z, TR), pl.ds(pl.multiple_of((2 * s + core) * W, W), W)]
        sends.append(send(part(1 - k), pt.at[s, table_rows], t_s.at[0, s], t_s.at[1, s], sibling))
        own = pltpu.make_async_copy(part(k), pt.at[s, table_rows], t_s.at[2, s])
        own.start()
        local.append(own)
    qb[xh, rows(z)] = q_in[...]
    idx[:, rows(z)] = idx_in[...]
    for turn_s, s in enumerate((xh, far)):
        owner = 2 * s + xh
        @pl.when(owner == x)
        def _():
            pt[s, rows(y)] = p_in[...]
        @pl.when(owner != x)
        def _():
            arrive(pt.at[s, rows(y)], p_r.at[s, y])
        for d in (1, 2, 3):
            sends.append(send(pt.at[s, rows(y)], pt.at[s, rows(y)], p_s.at[2 + turn_s * 3 + d - 1], p_r.at[s, y],
                              device(x, turn(y, d), z, k)))
    arrive(qb.at[far, rows(z)], q_r.at[far, z])
    for d in (1, 2, 3):
        sends.append(send(qb.at[far, rows(z)], qb.at[far, rows(z)], q_s.at[1, d], q_r.at[far, z],
                          device(x, y, turn(z, d), k)))
    for d in (1, 2, 3):
        arrive(idx.at[:, rows(turn(z, d))], i_r.at[turn(z, d)])

    first = xh * 512 + z * TR
    place = lax.broadcasted_iota(jnp.int32, (2 * TR, NB * R), 0)
    ids = (place + first + jnp.where(place >= TR, 256 - TR, 0)).astype(F32)
    count = jnp.zeros((2 * TR, NB * R), F32)
    for n in range(7):
        count += (idx[n:n + 1, :] == ids).astype(F32)

    for d in (1, 2, 3):
        for s in (xh, far):
            arrive(qb.at[s, rows(turn(z, d))], q_r.at[s, turn(z, d)])
            arrive(pt.at[s, rows(turn(y, d))], p_r.at[s, turn(y, d)])
    other_rows = pl.ds(NB * R + pl.multiple_of((1 - k) * TR, TR), TR)
    for s in range(2):
        arrive(pt.at[s, other_rows], t_s.at[1, s])
        local[s].wait()

    nt = (((1,), (1,)), ((), ()))
    for i in range(COLS // R):
        total = lax.dot_general(pt[0, i * R:(i + 1) * R], qb[0], nt, preferred_element_type=F32)
        total += lax.dot_general(pt[1, i * R:(i + 1) * R], qb[1], nt, preferred_element_type=F32)
        s_own[i * R:(i + 1) * R] = total
        sends.append(send(s_own.at[pl.ds(i * R, R)], s_far.at[pl.ds(i * R, R)], c_s.at[i], c_r.at[i], sibling))
    top = jnp.full((1, NB * R), -jnp.inf, F32)
    hit = jnp.zeros((1, NB * R), F32)
    positive = idx[7:8, :]
    base = xh * 2048 + z * R

    def here(i):
        return (lax.broadcasted_iota(jnp.int32, (R, NB * R), 0) + base + i * 512).astype(F32) == positive

    for i in range(COLS // R):
        arrive(s_far.at[pl.ds(i * R, R)], c_r.at[i])
        total = (s_own[i * R:(i + 1) * R] + s_far[i * R:(i + 1) * R]) * factor
        e_buf[i * R:(i + 1) * R] = total
        if i < NB:
            hit += jnp.sum(jnp.where(here(i), total, 0.0), axis=0, keepdims=True)
        else:
            total = jnp.where(count > 0, total, -jnp.inf)
        top = jnp.maximum(top, jnp.max(total, axis=0, keepdims=True))
    mass = jnp.zeros((1, NB * R), F32)
    for i in range(COLS // R):
        if i < NB:
            e = jnp.exp(e_buf[i * R:(i + 1) * R] - top)
        else:
            e = count * jnp.exp(jnp.where(count > 0, e_buf[i * R:(i + 1) * R] - top, 0.0))
        e_buf[i * R:(i + 1) * R] = e
        mass += jnp.sum(e, axis=0, keepdims=True)
    me = xh * 4 + z
    stats[me, 0:1] = top
    stats[me, 1:2] = mass
    stats[me, 2:3] = hit
    for n in range(1, 8):
        dx, d = n // 4, n % 4
        sends.append(send(stats.at[me], stats.at[me], st_s.at[n], st_r.at[me],
                          device(lax.rem(x + 2 * dx, 4), y, turn(z, d), k)))
    for n in range(1, 8):
        dx, d = n // 4, n % 4
        slot = lax.rem(xh + dx, 2) * 4 + turn(z, d)
        arrive(stats.at[slot], st_r.at[slot])
    row_top = stats[0, 0:1]
    for n in range(1, 8):
        row_top = jnp.maximum(row_top, stats[n, 0:1])
    mass = jnp.zeros((1, NB * R), F32)
    hit = jnp.zeros((1, NB * R), F32)
    for n in range(8):
        mass += stats[n, 1:2] * jnp.exp(stats[n, 0:1] - row_top)
        hit += stats[n, 2:3]
    log_total = row_top + jnp.log(mass)
    loss_out[...] = jnp.broadcast_to(log_total - hit, (8, NB * R))
    weight = idx[8:9, :] * factor
    scale = weight * jnp.exp(top - log_total)
    for i in range(COLS // R):
        g = scale * e_buf[i * R:(i + 1) * R]
        if i < NB:
            g = g - jnp.where(here(i), weight, 0.0)
        grad[i * R:(i + 1) * R] = g.astype(BF16)

    tn = (((0,), (0,)), ((), ()))

    def query_part(s, zz):
        return lax.dot_general(grad[:, rows(zz)], pt[s], tn, preferred_element_type=F32)

    def passage_part(s, i):
        return lax.dot_general(grad[rows(i)], qb[s], (((1,), (0,)), ((), ())), preferred_element_type=F32)

    def tile_sends(step, s):
        for d in (1, 2, 3):
            zz, yy = turn(z, d), turn(y, d)
            qg_part[step, d] = query_part(s, zz).astype(BF16)
            sends.append(send(qg_part.at[step, d], rq.at[step, 4 - d], qg_s.at[step, d], qg_r.at[step, 4 - d],
                              device(x, y, zz, k)))
            pg_part[step, d] = passage_part(s, yy).astype(BF16)
            sends.append(send(pg_part.at[step, d], rp.at[step, 4 - d], pg_s.at[step, d], pg_r.at[step, 4 - d],
                              device(x, yy, z, k)))

    tile_sends(0, far)
    tile_sends(1, xh)
    for s in range(2):
        tg_part[s] = lax.dot_general(grad[NB * R:], qb[s], (((1,), (0,)), ((), ())),
                                     preferred_element_type=F32).astype(BF16)
    for n in range(8):
        dx, d = n // 4, n % 4
        xx, yy = lax.rem(xl + dx, 2), turn(y, d)
        src = tg_part.at[xx, :, pl.ds(pl.multiple_of(yy * CW, CW), CW)]
        slot = dx * 4 + (4 - d) % 4
        if n:
            sends.append(send(src, rt.at[slot], tg_s.at[n], tg_r.at[slot], device(2 * xh + xx, yy, z, k)))
        else:
            own = pltpu.make_async_copy(src, rt.at[0], tg_s.at[0])
            own.start()
            local.append(own)
    qx[...] = query_part(far, z).astype(BF16)
    qg_out[...] = query_part(xh, z)
    px[0] = passage_part(far, y)
    px[1] = passage_part(xh, y)

    for d in (1, 2, 3):
        arrive(rq.at[0, d], qg_r.at[0, d])
    rq[0, 0] = (qx[...].astype(F32) + rq[0, 1].astype(F32) + rq[0, 2].astype(F32) + rq[0, 3].astype(F32)).astype(BF16)
    sends.append(send(rq.at[0, 0], rqx, qx_s.at[0], qx_s.at[1], device(opposite, y, z, k)))
    for step, s in enumerate((far, xh)):
        owner = 2 * s + xh
        for d in (1, 2, 3):
            arrive(rp.at[step, d], pg_r.at[step, d])
        total = px[step] + rp[step, 1].astype(F32) + rp[step, 2].astype(F32) + rp[step, 3].astype(F32)
        rp[step, 0] = total.astype(BF16)
        @pl.when(owner == x)
        def _():
            rpx[xl] = rp[step, 0]
        @pl.when(owner != x)
        def _():
            send(rp.at[step, 0], rpx.at[xl], px_s.at[step], px_r.at[xl], device(owner, y, z, k))

    local[2].wait()
    for n in range(1, 8):
        arrive(rt.at[n], tg_r.at[n])
    total = rt[0].astype(F32)
    for n in range(1, 8):
        total += rt[n].astype(F32)
    dst_y = 2 * k + lax.div(y, 2)
    for core in range(2):
        for h in range(2):
            tsum[core, h] = total[core * TR:(core + 1) * TR, h * 128:(h + 1) * 128]
            dst_z = 2 * lax.rem(y, 2) + h
            mine = (dst_y == y) & (dst_z == z) & (k == core)
            @pl.when(mine)
            def _():
                tt[z] = tsum[core, h]
            @pl.when(jnp.logical_not(mine))
            def _():
                send(tsum.at[core, h], tt.at[z], tt_s.at[core, h], tt_r.at[z], device(x, dst_y, dst_z, core))

    for d in (1, 2, 3):
        arrive(rq.at[1, d], qg_r.at[1, d])
    qg_out[...] += rq[1, 1].astype(F32) + rq[1, 2].astype(F32) + rq[1, 3].astype(F32)
    for zz in range(4):
        @pl.when(jnp.logical_not((src_y == y) & (src_k == k) & (z == zz)))
        def _():
            arrive(tt.at[zz], tt_r.at[zz])
        tg_out[zz * TR:(zz + 1) * TR] = tt[zz]
    arrive(rqx, qx_s.at[1])
    qg_out[...] += rqx[...].astype(F32)
    for t in range(2):
        @pl.when(x != 2 * xl + t)
        def _():
            arrive(rpx.at[t], px_r.at[t])
    pg_out[...] = rpx[0].astype(F32) + rpx[1].astype(F32)

    for copy in sends:
        copy.wait_send()

    def left(src, ss):
        pltpu.make_async_remote_copy(
            src_ref=src, dst_ref=src, send_sem=ss, recv_sem=ss, device_id=sibling, device_id_type=MESH
        ).wait_send()

    for t in range(2):
        @pl.when(x != 2 * xl + t)
        def _():
            left(p_in, p_s.at[t])
    for step, s in enumerate((far, xh)):
        @pl.when(2 * s + xh != x)
        def _():
            left(rp.at[step, 0], px_s.at[step])
    for core in range(2):
        for h in range(2):
            mine = (dst_y == y) & (2 * lax.rem(y, 2) + h == z) & (k == core)
            @pl.when(jnp.logical_not(mine))
            def _():
                left(tsum.at[core, h], tt_s.at[core, h])


def per_device(queries, passages, table, neg_owner, neg_row, positive, loss_weight):
    factor = float(queries.shape[1] * 4) ** (-0.5)
    ids = (neg_owner * 256 + neg_row).astype(F32).T
    idx = jnp.concatenate(
        [ids, positive.astype(F32)[None], loss_weight[None], jnp.zeros((7, R), F32)], axis=0
    )
    vmem = pl.BlockSpec(memory_space=pltpu.VMEM)
    dma = pltpu.SemaphoreType.DMA
    loss, qg, pg, tg = pl.pallas_call(
        functools.partial(kernel, factor),
        name="contrastive",
        out_shape=(
            jax.ShapeDtypeStruct((8, NB * R), F32),
            jax.ShapeDtypeStruct((R, W), F32),
            jax.ShapeDtypeStruct((R, W), F32),
            jax.ShapeDtypeStruct((4 * TR, 128), F32),
        ),
        in_specs=[vmem, vmem, pl.BlockSpec(memory_space=pl.ANY), vmem],
        out_specs=[vmem] * 4,
        scratch_shapes=[
            pltpu.VMEM((2, NB * R, W), BF16),
            pltpu.VMEM((2, COLS, W), BF16),
            pltpu.VMEM((16, NB * R), F32),
            pltpu.VMEM((COLS, NB * R), F32),
            pltpu.VMEM((COLS, NB * R), F32),
            pltpu.VMEM((COLS, NB * R), F32),
            pltpu.VMEM((COLS, NB * R), BF16),
            pltpu.VMEM((8, 8, NB * R), F32),
            pltpu.VMEM((2, 4, R, W), BF16),
            pltpu.VMEM((2, 4, R, W), BF16),
            pltpu.VMEM((2, 2 * TR, W), BF16),
            pltpu.VMEM((2, 4, R, W), BF16),
            pltpu.VMEM((R, W), BF16),
            pltpu.VMEM((2, 4, R, W), BF16),
            pltpu.VMEM((2, R, W), BF16),
            pltpu.VMEM((8, 2 * TR, CW), BF16),
            pltpu.VMEM((4, TR, 128), F32),
            pltpu.VMEM((R, W), BF16),
            pltpu.VMEM((2, R, W), F32),
            pltpu.VMEM((2, 2, TR, 128), F32),
            dma((2, 4)), dma((2, 4)),
            dma((8,)), dma((2, 4)),
            dma((3, 2)),
            dma((4,)), dma((4,)),
            dma((5,)), dma((5,)),
            dma((8,)), dma((8,)),
            dma((2, 4)), dma((2, 4)),
            dma((2,)),
            dma((2, 4)), dma((2, 4)),
            dma((2,)), dma((2,)),
            dma((8,)), dma((8,)),
            dma((2, 2)), dma((4,)),
        ],
        compiler_params=pltpu.CompilerParams(
            collective_id=0, has_side_effects=True, vmem_limit_bytes=48 * 2**20
        ),
    )(queries, passages, table, idx)
    start = lax.rem(lax.axis_index("blk"), 4) * R + lax.axis_index("corpus") * 32
    return lax.dynamic_slice(loss[0], (start,), (32,)), qg, pg, tg


def solution(mesh):
    placed = (
        P("blk", "corpus"),
        P("blk", "corpus"),
        P("corpus", None),
        P("blk", None),
        P("blk", None),
        P("blk"),
        P("blk"),
    )
    return jax.shard_map(
        per_device,
        mesh=mesh,
        in_specs=placed,
        out_specs=(
            P(("blk", "corpus")),
            P("blk", "corpus"),
            P("blk", "corpus"),
            P("corpus", "blk"),
        ),
        check_vma=False,
    )
```

time: 739 us -> 97.6 us (0.13)
  waiting for transfers between devices: 546 us -> 0 us
  Pallas kernels: 0 us -> 86.9 us
  blocking collectives: 60.1 us -> 0 us
  other arithmetic: 50.3 us -> 2.09 us
  matrix products: 30.1 us -> 0 us
  local copies, waits for them, and re-layouts: 33.1 us -> 6.4 us
  between operations: 14 us -> 0.67 us
    reduce_scatter x2 -> x0, waiting for transfers between devices: 351 us -> none  [the longest x1 203 us: per_device(): lax.psum_scatter(lax.dot_general(soft_grad, queries, (((0,), (0,)), ((),...]
    all_gather x1 -> x0, waiting for transfers between devices: 158 us -> none  [per_device(): all_passages = lax.all_gather(passages, 'blk', axis=0, tiled=True)]
    pallas_call x0 -> x1, Pallas kernels: none -> 86.9 us  [per_device(): pl.pallas_call(functools.partial(kernel, factor), name='contrastive', out...]
    all_to_all x1 -> x0, blocking collectives: 52.2 us -> none  [per_device(): lax.all_to_all(dense_grad, 'corpus', split_axis=0, concat_axis=1, tiled=T...]
    scatter-add x1 -> x0, other arithmetic: 44.6 us -> none  [per_device(): mixing = jnp.zeros((table_rows, q_rows), jnp.float32).at[flat_ids, query_...]
    psum x1 -> x0, waiting for transfers between devices: 35.9 us -> none  [per_device(): logits, hard_logits = lax.psum((logits, hard_logits), 'corpus')]
    dot_general x7 -> x0, matrix products: 30.1 us -> none  [the longest x1 9.92 us: per_device(): lax.dot_general(soft_grad, queries, (((0,), (0,)), ((), ())), preferred_e...]
    gather x2 -> x0, local copies, waits for them, and re-layouts: 12.3 us -> none  [the longest x1 8.05 us: per_device(): picked = arrived[slot_index]]
  transfers between devices with their start and end apart: 5 -> 0, of which waited for: 4 -> 0; matrix products, arithmetic and copies ran while one was open for 8% -> 0% of each run, Pallas kernels for 0% -> 0%
where the time goes in v1:
time: 97.6 us; the launch traced here: 96.1 us
  Pallas kernels  86.9 us (89%)
  local copies, waits for them, and re-layouts  6.4 us (7%)
  other arithmetic  2.09 us (2%)
    pallas_call x1, Pallas kernels, per_device(): pl.pallas_call(functools.partial(kernel, factor), name='contrastive', out...  86.9 us
    unnamed x9, local copies, waits for them, and re-layouts  5.73 us

profile of v1, /device:TPU:0, one launch (start us, length us, event | category | flops | bytes accessed | tf_op | source)
XLA Modules:
  0.0 96.1 jit_solution(15030072469184509783)
XLA Ops:
  0.6 0.7 convert_bitcast_fusion.1
  1.3 0.1 pad.3.clone
  1.4 0.7 convert_bitcast_fusion
  2.1 0.7 maximum_maximum_fusion.idx_in
  2.8 0.0 copy-start
  2.8 1.6 %copy-done = bf16[256,4096]{1,0:T(8,128)(2,1)S(1)} copy-done((bf16[256,4096]{1,0:T(8,128)(2,1)S(1)}, bf16[256,4096]{1,0:T(8,128)(2,1)}, u32[]{:S(2)}) %copy-start) | copy-done | bytes 2097176
  4.4 0.0 copy-start.1
  4.4 0.9 copy-done.1
  5.4 0.0 copy-start.2
  5.4 0.9 copy-done.2
  6.3 86.9 %contrastive.1 = (f32[8,512]{1,0:T(8,128)S(1)}, f32[128,1024]{1,0:T(8,128)S(1)}, f32[128,1024]{1,0:T(8,128)S(1)}, f32[256,128]{1,0:T(8,128)S(1)}) custom-call(bf16[128,1024]{1,0:T(8,128)(2,1)S(1)} %copy-done.1, bf16[128,1024]{1,0:T(8,128)(2,1)S(1)} %copy-done.2, bf16[256,4096]{1,0:T(8,128)(2,1)S(1)} %copy-done, f32[16,128]{1,0:T(8,128)S(1)} %maximum_maximum_fusion.idx_in), custom_call_target="tpu_custom_call" | custom-call | tf_op jit(solution)/shard_map/contrastive/pallas_call | solution.py:314
  93.2 0.6 dynamic-slice_bitcast_fusion
  93.8 0.8 copy.14
  94.6 0.8 copy.15
  95.4 0.7 copy.16
  (2 shorter events, 0.0 us)
Async XLA Ops:
  2.8 1.6 %copy-start = (bf16[256,4096]{1,0:T(8,128)(2,1)S(1)}, bf16[256,4096]{1,0:T(8,128)(2,1)}, u32[]{:S(2)}) copy-start(bf16[256,4096]{1,0:T(8,128)(2,1)} %t_in.1) | copy-start | bytes 6291460
  4.4 0.9 copy-start.1
  5.4 0.9 copy-start.2

commit v2 on v1

v2 whole, which is shorter than its diff:
```python
import functools

import jax
import jax.numpy as jnp
from jax import lax
from jax.experimental import pallas as pl
from jax.experimental.pallas import tpu as pltpu
from jax.sharding import PartitionSpec as P

MESH = pl.DeviceIdType.MESH
F32 = jnp.float32
BF16 = jnp.bfloat16

R = 128
H = 64
W = 1024
NB = 4
TR = 64
COLS = NB * R + 2 * TR
CW = 256


def device(x, y, z, k):
    return (lax.rem(x, 2) * 16 + y * 4 + z, lax.div(x, 2) * 2 + k)


def kernel(
    factor, q_in, p_in, t_in, owner_in, row_in, pos_in, weight_in, loss_out, qg_out, pg_out, tg_out,
    qb, pt, idx, s_own, s_far, e_buf, grad, stats, qg_part, pg_part, tg_part,
    rq, rqx, rp, rpx, rt, rtx, tt, qx, px, tx, tsum, p_buf, owner_buf, row_buf, pos_buf, weight_buf, loss_row,
    in_s, q_s, q_r, px_s, p_s, p_r, t_s, i_s, i_r, c_s, c_r, st_s, st_r,
    qg_s, qg_r, qx_s, pg_s, pg_r, sx_s, sx_r, tx_s, tg_s, tg_r, tt_s, tt_r,
):
    b, c = lax.axis_index("blk"), lax.axis_index("corpus")
    xl, y, z = lax.div(b, 16), lax.rem(lax.div(b, 4), 4), lax.rem(b, 4)
    xh, k = lax.div(c, 2), lax.rem(c, 2)
    x = 2 * xh + xl
    far, yon = 1 - xh, 1 - xl
    opposite = 2 * far + xl
    sibling = device(x, y, z, 1 - k)

    def send(src, dst, ss, rs, where):
        copy = pltpu.make_async_remote_copy(
            src_ref=src, dst_ref=dst, send_sem=ss, recv_sem=rs, device_id=where, device_id_type=MESH
        )
        copy.start()
        sends.append(copy)

    def arrive(dst, rs):
        pltpu.make_async_remote_copy(
            src_ref=dst, dst_ref=dst, send_sem=rs, recv_sem=rs, device_id=sibling, device_id_type=MESH
        ).wait_recv()

    def stage(src, dst, sem):
        copy = pltpu.make_async_copy(src, dst, sem)
        copy.start()
        return copy

    def turn(v, d):
        return lax.rem(v + d, 4)

    def rows(i, n=R):
        return pl.ds(pl.multiple_of(i * n, n), n)

    def half(l, yy):
        return rows(l * 4 + yy, H)

    sends = []
    barrier = pltpu.get_barrier_semaphore()
    peers = [sibling]
    for d in (1, 2, 3):
        peers.append(device(turn(x, d), y, z, k))
        peers.append(device(x, turn(y, d), z, k))
        peers.append(device(x, y, turn(z, d), k))
    for peer in peers:
        pl.semaphore_signal(barrier, 1, device_id=peer, device_id_type=MESH)

    table_rows = pl.ds(NB * R + pl.multiple_of(k * TR, TR), TR)
    own = [
        stage(p_in, p_buf, in_s.at[0]),
        stage(q_in, qb.at[xh, rows(z)], in_s.at[1]),
        stage(owner_in, owner_buf, in_s.at[2]),
        stage(row_in, row_buf, in_s.at[3]),
        stage(pos_in, pos_buf, in_s.at[4]),
        stage(weight_in, weight_buf, in_s.at[5]),
    ]

    def table_part(s, core):
        return t_in.at[rows(z, TR), pl.ds(pl.multiple_of((2 * s + core) * W, W), W)]

    own_table = [stage(table_part(s, k), pt.at[s, table_rows], in_s.at[6 + s]) for s in range(2)]
    for copy in own:
        copy.wait()
    pt[xh, half(xl, y)] = p_buf[rows(xh, H)]
    idx[0:7, rows(z)] = (owner_buf[...] * 256 + row_buf[...]).astype(F32)
    idx[7:8, rows(z)] = pos_buf[...].astype(F32)
    idx[8:9, rows(z)] = weight_buf[...]
    pl.semaphore_wait(barrier, len(peers))

    send(p_buf.at[rows(xh, H)], pt.at[xh, half(xl, y)], px_s.at[0], p_r.at[xh, xl, y], device(2 * xh + yon, y, z, k))
    send(p_buf.at[rows(far, H)], pt.at[xh, half(xl, y)], px_s.at[1], p_r.at[xh, xl, y], device(2 * far + yon, y, z, k))
    send(p_buf.at[rows(far, H)], pt.at[xh, half(xl, y)], px_s.at[2], p_r.at[xh, xl, y], device(opposite, y, z, k))

    def spread_passages(n, s, l):
        for d in (1, 2, 3):
            send(pt.at[s, half(l, y)], pt.at[s, half(l, y)], p_s.at[n, d], p_r.at[s, l, y], device(x, turn(y, d), z, k))

    def spread_queries(n, s):
        for d in (1, 2, 3):
            send(qb.at[s, rows(z)], qb.at[s, rows(z)], q_s.at[n, d], q_r.at[s, z], device(x, y, turn(z, d), k))

    spread_passages(0, xh, xl)
    spread_queries(0, xh)
    send(qb.at[xh, rows(z)], qb.at[xh, rows(z)], q_s.at[0, 0], q_r.at[xh, z], device(opposite, y, z, k))
    for d in (1, 2, 3):
        send(idx.at[:, rows(z)], idx.at[:, rows(z)], i_s.at[d], i_r.at[z], device(x, y, turn(z, d), k))
    for s in range(2):
        send(table_part(s, 1 - k), pt.at[s, table_rows], t_s.at[0, s], t_s.at[1, s], sibling)
    for n, (s, l) in enumerate(((xh, yon), (far, yon), (far, xl))):
        arrive(pt.at[s, half(l, y)], p_r.at[s, l, y])
        spread_passages(n + 1, s, l)
    arrive(qb.at[far, rows(z)], q_r.at[far, z])
    spread_queries(1, far)
    for d in (1, 2, 3):
        arrive(idx.at[:, rows(turn(z, d))], i_r.at[turn(z, d)])

    first = xh * 512 + z * TR
    place = lax.broadcasted_iota(jnp.int32, (2 * TR, NB * R), 0)
    named = (place + first + jnp.where(place >= TR, 256 - TR, 0)).astype(F32)
    count = jnp.zeros((2 * TR, NB * R), F32)
    for n in range(7):
        count += (idx[n:n + 1, :] == named).astype(F32)

    other_rows = pl.ds(NB * R + pl.multiple_of((1 - k) * TR, TR), TR)
    for s in range(2):
        arrive(pt.at[s, other_rows], t_s.at[1, s])
        own_table[s].wait()
    nt = (((1,), (1,)), ((), ()))
    for s in (xh, far):
        for d in (1, 2, 3):
            arrive(qb.at[s, rows(turn(z, d))], q_r.at[s, turn(z, d)])
            for l in (xl, yon):
                arrive(pt.at[s, half(l, turn(y, d))], p_r.at[s, l, turn(y, d)])
        for i in range(COLS // R):
            term = lax.dot_general(pt[s, i * R:(i + 1) * R], qb[s], nt, preferred_element_type=F32)
            if s is xh:
                s_own[i * R:(i + 1) * R] = term
            else:
                s_own[i * R:(i + 1) * R] += term
                send(s_own.at[pl.ds(i * R, R)], s_far.at[pl.ds(i * R, R)], c_s.at[i], c_r.at[i], sibling)
    top = jnp.full((1, NB * R), -jnp.inf, F32)
    hit = jnp.zeros((1, NB * R), F32)
    positive = idx[7:8, :]

    def here(i):
        r = lax.broadcasted_iota(jnp.int32, (R, NB * R), 0)
        r = r + jnp.where(r >= H, 4 * R - H, 0) + (i // 2 * 2048 + i % 2 * 1024) + z * R + xh * H
        return r.astype(F32) == positive

    for i in range(COLS // R):
        arrive(s_far.at[pl.ds(i * R, R)], c_r.at[i])
        total = (s_own[i * R:(i + 1) * R] + s_far[i * R:(i + 1) * R]) * factor
        e_buf[i * R:(i + 1) * R] = total
        if i < NB:
            hit += jnp.sum(jnp.where(here(i), total, 0.0), axis=0, keepdims=True)
        else:
            total = jnp.where(count > 0, total, -jnp.inf)
        top = jnp.maximum(top, jnp.max(total, axis=0, keepdims=True))
    mass = jnp.zeros((1, NB * R), F32)
    for i in range(COLS // R):
        if i < NB:
            e = jnp.exp(e_buf[i * R:(i + 1) * R] - top)
        else:
            e = count * jnp.exp(jnp.where(count > 0, e_buf[i * R:(i + 1) * R] - top, 0.0))
        e_buf[i * R:(i + 1) * R] = e
        mass += jnp.sum(e, axis=0, keepdims=True)
    me = xh * 4 + z
    stats[me, 0:1] = top
    stats[me, 1:2] = mass
    stats[me, 2:3] = hit
    for n in range(1, 8):
        dx, d = n // 4, n % 4
        send(stats.at[me], stats.at[me], st_s.at[n], st_r.at[me], device(turn(x, 2 * dx), y, turn(z, d), k))
    for n in range(1, 8):
        dx, d = n // 4, n % 4
        slot = lax.rem(xh + dx, 2) * 4 + turn(z, d)
        arrive(stats.at[slot], st_r.at[slot])
    row_top = stats[0, 0:1]
    for n in range(1, 8):
        row_top = jnp.maximum(row_top, stats[n, 0:1])
    mass = jnp.zeros((1, NB * R), F32)
    hit = jnp.zeros((1, NB * R), F32)
    for n in range(8):
        mass += stats[n, 1:2] * jnp.exp(stats[n, 0:1] - row_top)
        hit += stats[n, 2:3]
    log_total = row_top + jnp.log(mass)
    loss_row[...] = log_total - hit
    own_loss = jnp.broadcast_to(loss_row[:, rows(z)], (8, R))
    loss_out[...] = pltpu.roll(own_loss, lax.rem(R - c * 32, R), 1)
    weight = idx[8:9, :] * factor
    scale = weight * jnp.exp(top - log_total)
    for i in range(COLS // R):
        g = scale * e_buf[i * R:(i + 1) * R]
        if i < NB:
            g = g - jnp.where(here(i), weight, 0.0)
        grad[i * R:(i + 1) * R] = g.astype(BF16)

    nn, tn = (((1,), (0,)), ((), ())), (((0,), (0,)), ((), ()))

    def query_part(s, zz):
        return lax.dot_general(grad[:, rows(zz)], pt[s], tn, preferred_element_type=F32)

    def query_sends(step, s):
        for d in (1, 2, 3):
            zz = turn(z, d)
            qg_part[step, d] = query_part(s, zz).astype(BF16)
            send(qg_part.at[step, d], rq.at[step, 4 - d], qg_s.at[step, d], qg_r.at[step, 4 - d], device(x, y, zz, k))

    def passage_sends(n, s, l):
        part = lax.dot_general(grad[rows(l, 4 * H)], qb[s], nn, preferred_element_type=F32)
        pg_part[n] = part.astype(BF16)
        px[n] = part
        for d in (1, 2, 3):
            yy = turn(y, d)
            send(pg_part.at[n, rows(yy, H)], rp.at[n, 4 - d], pg_s.at[n, d], pg_r.at[n, 4 - d], device(x, yy, z, k))

    def table_half(l):
        return lax.dot_general(grad[NB * R:], qb[l], nn, preferred_element_type=F32)

    order = ((far, xl), (far, yon), (xh, yon), (xh, xl))
    tg_part[0] = table_half(yon).astype(BF16)
    send(tg_part.at[0], rtx, tx_s.at[0], tx_s.at[1], device(2 * xh + yon, y, z, k))
    passage_sends(0, *order[0])
    query_sends(0, far)
    passage_sends(1, *order[1])
    passage_sends(2, *order[2])
    query_sends(1, xh)
    passage_sends(3, *order[3])
    tx[...] = table_half(xl)
    qx[...] = query_part(far, z)
    qg_out[...] = query_part(xh, z)

    arrive(rtx, tx_s.at[1])
    tx[...] += rtx[...].astype(F32)
    tg_part[1] = tx[...].astype(BF16)
    for d in (1, 2, 3):
        yy = turn(y, d)
        send(tg_part.at[1, :, rows(yy, CW)], rt.at[4 - d], tg_s.at[d], tg_r.at[4 - d], device(x, yy, z, k))

    def passage_sum(n):
        total = px[n, rows(y, H)]
        for d in (1, 2, 3):
            arrive(rp.at[n, d], pg_r.at[n, d])
            total += rp[n, d].astype(F32)
        return total

    def passage_on(n):
        s, l = order[n]
        rp[n, 0] = passage_sum(n).astype(BF16)
        send(rp.at[n, 0], rpx.at[xh, xl], sx_s.at[n], sx_r.at[xh, xl], device(2 * s + l, y, z, k))

    passage_on(0)
    total = qx[...]
    for d in (1, 2, 3):
        arrive(rq.at[0, d], qg_r.at[0, d])
        total += rq[0, d].astype(F32)
    rq[0, 0] = total.astype(BF16)
    send(rq.at[0, 0], rqx, qx_s.at[0], qx_s.at[1], device(opposite, y, z, k))
    passage_on(1)
    passage_on(2)

    total = tx[:, rows(y, CW)]
    for d in (1, 2, 3):
        arrive(rt.at[d], tg_r.at[d])
        total += rt[d].astype(F32)
    dst_y = 2 * k + lax.div(y, 2)
    for core in range(2):
        for h in range(2):
            tsum[core, h] = total[core * TR:(core + 1) * TR, h * 128:(h + 1) * 128]
            dst_z = 2 * lax.rem(y, 2) + h
            mine = (dst_y == y) & (dst_z == z) & (k == core)

            @pl.when(mine)
            def _():
                tt[z] = tsum[core, h]

            @pl.when(jnp.logical_not(mine))
            def _():
                send(tsum.at[core, h], tt.at[z], tt_s.at[core, h], tt_r.at[z], device(x, dst_y, dst_z, core))
                sends.pop()

    total = qg_out[...]
    for d in (1, 2, 3):
        arrive(rq.at[1, d], qg_r.at[1, d])
        total += rq[1, d].astype(F32)
    arrive(rqx, qx_s.at[1])
    qg_out[...] = total + rqx[...].astype(F32)
    total = passage_sum(3)
    arrive(rpx.at[xh, yon], sx_r.at[xh, yon])
    pg_out[rows(xh, H)] = total + rpx[xh, yon].astype(F32)
    for l in range(2):
        arrive(rpx.at[far, l], sx_r.at[far, l])
    pg_out[rows(far, H)] = rpx[far, 0].astype(F32) + rpx[far, 1].astype(F32)
    src_y = 2 * lax.rem(y, 2) + lax.div(z, 2)
    src_k = lax.div(y, 2)
    for zz in range(4):
        @pl.when(jnp.logical_not((src_y == y) & (src_k == k) & (z == zz)))
        def _():
            arrive(tt.at[zz], tt_r.at[zz])

        tg_out[zz * TR:(zz + 1) * TR] = tt[zz]

    for copy in sends:
        copy.wait_send()
    for core in range(2):
        for h in range(2):
            mine = (dst_y == y) & (2 * lax.rem(y, 2) + h == z) & (k == core)

            @pl.when(jnp.logical_not(mine))
            def _():
                src, sem = tsum.at[core, h], tt_s.at[core, h]
                pltpu.make_async_remote_copy(
                    src_ref=src, dst_ref=src, send_sem=sem, recv_sem=sem, device_id=sibling, device_id_type=MESH
                ).wait_send()


def place(loss_in, qg_in, pg_in, tg_in, loss_out, qg_out, pg_out, tg_out, sem):
    copies = []
    for n, (src, dst) in enumerate(((qg_in, qg_out), (pg_in, pg_out), (tg_in, tg_out))):
        copies.append(pltpu.make_async_copy(src, dst, sem.at[n]))
        copies[-1].start()
    loss_out[...] = loss_in[0:1, 0:32]
    for copy in copies:
        copy.wait()


def per_device(queries, passages, table, neg_owner, neg_row, positive, loss_weight):
    factor = float(queries.shape[1] * 4) ** (-0.5)
    vmem = pl.BlockSpec(memory_space=pltpu.VMEM)
    dma = pltpu.SemaphoreType.DMA
    loss, qg, pg, tg = pl.pallas_call(
        functools.partial(kernel, factor),
        name="contrastive",
        out_shape=(
            pltpu.VMEM((8, R), F32),
            pltpu.VMEM((R, W), F32),
            pltpu.VMEM((R, W), F32),
            pltpu.VMEM((4 * TR, 128), F32),
        ),
        in_specs=[pl.BlockSpec(memory_space=pl.ANY)] * 7,
        out_specs=[vmem] * 4,
        scratch_shapes=[
            pltpu.VMEM((2, NB * R, W), BF16),
            pltpu.VMEM((2, COLS, W), BF16),
            pltpu.VMEM((16, NB * R), F32),
            pltpu.VMEM((COLS, NB * R), F32),
            pltpu.VMEM((COLS, NB * R), F32),
            pltpu.VMEM((COLS, NB * R), F32),
            pltpu.VMEM((COLS, NB * R), BF16),
            pltpu.VMEM((8, 8, NB * R), F32),
            pltpu.VMEM((2, 4, R, W), BF16),
            pltpu.VMEM((4, 4 * H, W), BF16),
            pltpu.VMEM((2, 2 * TR, W), BF16),
            pltpu.VMEM((2, 4, R, W), BF16),
            pltpu.VMEM((R, W), BF16),
            pltpu.VMEM((4, 4, H, W), BF16),
            pltpu.VMEM((2, 2, H, W), BF16),
            pltpu.VMEM((4, 2 * TR, CW), BF16),
            pltpu.VMEM((2 * TR, W), BF16),
            pltpu.VMEM((4, TR, 128), F32),
            pltpu.VMEM((R, W), F32),
            pltpu.VMEM((4, 4 * H, W), F32),
            pltpu.VMEM((2 * TR, W), F32),
            pltpu.VMEM((2, 2, TR, 128), F32),
            pltpu.VMEM((R, W), BF16),
            pltpu.VMEM((7, R), jnp.int32),
            pltpu.VMEM((7, R), jnp.int32),
            pltpu.VMEM((1, R), jnp.int32),
            pltpu.VMEM((1, R), F32),
            pltpu.VMEM((1, NB * R), F32),
            dma((8,)),
            dma((2, 4)), dma((2, 4)),
            dma((3,)), dma((4, 4)), dma((2, 2, 4)),
            dma((2, 2)),
            dma((4,)), dma((4,)),
            dma((5,)), dma((5,)),
            dma((8,)), dma((8,)),
            dma((2, 4)), dma((2, 4)),
            dma((2,)),
            dma((4, 4)), dma((4, 4)),
            dma((3,)), dma((2, 2)),
            dma((2,)), dma((4,)), dma((4,)),
            dma((2, 2)), dma((4,)),
        ],
        compiler_params=pltpu.CompilerParams(
            collective_id=0, has_side_effects=True, vmem_limit_bytes=48 * 2**20
        ),
    )(*[
        pltpu.with_memory_space_constraint(a, pltpu.HBM)
        for a in (queries, passages, table, neg_owner.T, neg_row.T, positive[None], loss_weight[None])
    ])
    loss, qg, pg, tg = pl.pallas_call(
        place,
        name="place",
        out_shape=(
            jax.ShapeDtypeStruct((1, 32), F32),
            jax.ShapeDtypeStruct((R, W), F32),
            jax.ShapeDtypeStruct((R, W), F32),
            jax.ShapeDtypeStruct((4 * TR, 128), F32),
        ),
        in_specs=[vmem] + [pl.BlockSpec(memory_space=pl.ANY)] * 3,
        out_specs=[vmem] + [pl.BlockSpec(memory_space=pl.ANY)] * 3,
        scratch_shapes=[dma((3,))],
    )(*[pltpu.with_memory_space_constraint(a, pltpu.VMEM) for a in (loss, qg, pg, tg)])
    return loss[0], qg, pg, tg


def solution(mesh):
    placed = (
        P("blk", "corpus"),
        P("blk", "corpus"),
        P("corpus", None),
        P("blk", None),
        P("blk", None),
        P("blk"),
        P("blk"),
    )
    return jax.shard_map(
        per_device,
        mesh=mesh,
        in_specs=placed,
        out_specs=(
            P(("blk", "corpus")),
            P("blk", "corpus"),
            P("blk", "corpus"),
            P("corpus", "blk"),
        ),
        check_vma=False,
    )
```

time: 97.6 us -> 80.3 us (0.82)
  Pallas kernels: 86.9 us -> 78.1 us
  local copies, waits for them, and re-layouts: 6.4 us -> 0 us
  other arithmetic: 2.09 us -> 0 us
    pallas_call x1, Pallas kernels: 86.9 us -> 76.6 us  [per_device(): pl.pallas_call(functools.partial(kernel, factor), name='contrastive', out...]
    unnamed x9 -> x0, local copies, waits for them, and re-layouts: 5.73 us -> none
    pallas_call x0 -> x1, Pallas kernels: none -> 1.54 us  [per_device(): pl.pallas_call(place, name='place', out_shape=(jax.ShapeDtypeStruct((1, 3...]
where the time goes in v2:
time: 80.3 us; the launch traced here: 78.7 us
  Pallas kernels  78.1 us (97%)
    pallas_call x1, Pallas kernels, per_device(): pl.pallas_call(functools.partial(kernel, factor), name='contrastive', out...  76.6 us

profile of v2, /device:TPU:0, one launch (start us, length us, event | category | flops | bytes accessed | tf_op | source)
XLA Modules:
  0.0 78.7 jit_solution(712527321724682717)
XLA Ops:
  0.6 76.6 %contrastive.1 = (f32[8,128]{1,0:T(8,128)S(1)}, f32[128,1024]{1,0:T(8,128)S(1)}, f32[128,1024]{1,0:T(8,128)S(1)}, f32[256,128]{1,0:T(8,128)S(1)}) custom-call(bf16[128,1024]{1,0:T(8,128)(2,1)} %q_in.1, bf16[128,1024]{1,0:T(8,128)(2,1)} %p_in.1, bf16[256,4096]{1,0:T(8,128)(2,1)} %t_in.1, s32[7,128]{1,0:T(8,128)} %bitcast.5, s32[7,128]{1,0:T(8,128)} %bitcast.6, ...), custom_call_target="tpu_custom_call" | custom-call | tf_op jit(solution)/shard_map/contrastive/pallas_call | solution.py:341
  77.2 1.5 %place.1 = (f32[1,32]{1,0:T(1,128)}, f32[128,1024]{1,0:T(8,128)}, f32[128,1024]{1,0:T(8,128)}, f32[256,128]{1,0:T(8,128)}) custom-call(f32[8,128]{1,0:T(8,128)S(1)} %get-tuple-element.12.loss_in, f32[128,1024]{1,0:T(8,128)S(1)} %get-tuple-element.13.qg_in, f32[128,1024]{1,0:T(8,128)S(1)} %get-tuple-element.14.pg_in, f32[256,128]{1,0:T(8,128)S(1)} %get-tuple-element.15.tg_in), custom_call_target="tpu_custom_call" | custom-call | tf_op jit(solution)/shard_map/place/pallas_call | solution.py:402

commit v3 on v2

--- a/solution.py
+++ b/solution.py
@@ -27,8 +27,8 @@
 def kernel(
     factor, q_in, p_in, t_in, owner_in, row_in, pos_in, weight_in, loss_out, qg_out, pg_out, tg_out,
     qb, pt, idx, s_own, s_far, e_buf, grad, stats, qg_part, pg_part, tg_part,
-    rq, rqx, rp, rpx, rt, rtx, tt, qx, px, tx, tsum, p_buf, owner_buf, row_buf, pos_buf, weight_buf, loss_row,
-    in_s, q_s, q_r, px_s, p_s, p_r, t_s, i_s, i_r, c_s, c_r, st_s, st_r,
+    qg_on, pg_on, rqa, rpa, qg_sum, pg_sum, rq, rqx, rp, rpx, rt, rtx, tt, qx, px, tx, tsum, p_buf, owner_buf, row_buf, pos_buf, weight_buf, loss_row,
+    in_s, q_s, q_r, px_s, px_r, p_s, p_r, t_s, i_s, i_r, c_s, c_r, st_s, st_r,
     qg_s, qg_r, qx_s, pg_s, pg_r, sx_s, sx_r, tx_s, tg_s, tg_r, tt_s, tt_r,
 ):
     b, c = lax.axis_index("blk"), lax.axis_index("corpus")
@@ -97,30 +97,60 @@
     idx[8:9, rows(z)] = weight_buf[...]
     pl.semaphore_wait(barrier, len(peers))
 
-    send(p_buf.at[rows(xh, H)], pt.at[xh, half(xl, y)], px_s.at[0], p_r.at[xh, xl, y], device(2 * xh + yon, y, z, k))
-    send(p_buf.at[rows(far, H)], pt.at[xh, half(xl, y)], px_s.at[1], p_r.at[xh, xl, y], device(2 * far + yon, y, z, k))
-    send(p_buf.at[rows(far, H)], pt.at[xh, half(xl, y)], px_s.at[2], p_r.at[xh, xl, y], device(opposite, y, z, k))
-
-    def spread_passages(n, s, l):
-        for d in (1, 2, 3):
-            send(pt.at[s, half(l, y)], pt.at[s, half(l, y)], p_s.at[n, d], p_r.at[s, l, y], device(x, turn(y, d), z, k))
-
-    def spread_queries(n, s):
-        for d in (1, 2, 3):
-            send(qb.at[s, rows(z)], qb.at[s, rows(z)], q_s.at[n, d], q_r.at[s, z], device(x, y, turn(z, d), k))
-
-    spread_passages(0, xh, xl)
-    spread_queries(0, xh)
-    send(qb.at[xh, rows(z)], qb.at[xh, rows(z)], q_s.at[0, 0], q_r.at[xh, z], device(opposite, y, z, k))
+    def passages(s, l, d, part=None):
+        return pt.at[s, half(l, turn(y, d)) if part is None else rows((l * 4 + turn(y, d)) * 2 + part, H // 2)]
+
+    def queries(s, d, part=None):
+        return qb.at[s, rows(turn(z, d)) if part is None else rows(turn(z, d) * 2 + part, R // 2)]
+
+    def spread(block, ss, rs, forward, back):
+        send(block(0), block(0), ss.at[1], rs.at[1], forward)
+        send(block(0), block(0), ss.at[3], rs.at[3], back)
+
+    def relay(block, ss, rs, forward, back):
+        arrive(block(3), rs.at[1])
+        send(block(3, 0), block(3, 0), ss.at[0], rs.at[0], forward)
+        arrive(block(1), rs.at[3])
+        send(block(1, 1), block(1, 1), ss.at[2], rs.at[2], back)
+
+    def finish(block, rs):
+        arrive(block(2, 0), rs.at[0])
+        arrive(block(2, 1), rs.at[2])
+
+    y_next, y_last = device(x, turn(y, 1), z, k), device(x, turn(y, 3), z, k)
+    z_next, z_last = device(x, y, turn(z, 1), k), device(x, y, turn(z, 3), k)
+
+    def on_y(step, s, l):
+        step(functools.partial(passages, s, l), p_s.at[s, l], p_r.at[s, l], y_next, y_last)
+
+    def on_z(step, s):
+        step(functools.partial(queries, s), q_s.at[s], q_r.at[s], z_next, z_last)
+
+    def first_sends():
+        mine = pt.at[xh, half(xl, y)]
+        send(p_buf.at[rows(xh, H)], mine, px_s.at[0], px_r.at[xh, xl], device(2 * xh + yon, y, z, k))
+        send(p_buf.at[rows(far, H)], mine, px_s.at[1], px_r.at[xh, xl], device(2 * far + yon, y, z, k))
+        on_y(spread, xh, xl)
+        on_z(spread, xh)
+        send(queries(xh, 0), queries(xh, 0), qx_s.at[2], qx_s.at[3], device(opposite, y, z, k))
+        send(p_buf.at[rows(far, H)], mine, px_s.at[2], px_r.at[xh, xl], device(opposite, y, z, k))
+
+    first_sends()
     for d in (1, 2, 3):
         send(idx.at[:, rows(z)], idx.at[:, rows(z)], i_s.at[d], i_r.at[z], device(x, y, turn(z, d), k))
     for s in range(2):
         send(table_part(s, 1 - k), pt.at[s, table_rows], t_s.at[0, s], t_s.at[1, s], sibling)
-    for n, (s, l) in enumerate(((xh, yon), (far, yon), (far, xl))):
-        arrive(pt.at[s, half(l, y)], p_r.at[s, l, y])
-        spread_passages(n + 1, s, l)
-    arrive(qb.at[far, rows(z)], q_r.at[far, z])
-    spread_queries(1, far)
+    for s in (xh, far):
+        arrive(passages(s, yon, 0), px_r.at[s, yon])
+        on_y(spread, s, yon)
+    on_y(relay, xh, xl)
+    on_z(relay, xh)
+    on_y(relay, xh, yon)
+    arrive(queries(far, 0), qx_s.at[3])
+    on_z(spread, far)
+    on_y(relay, far, yon)
+    arrive(passages(far, xl, 0), px_r.at[far, xl])
+    on_y(spread, far, xl)
     for d in (1, 2, 3):
         arrive(idx.at[:, rows(turn(z, d))], i_r.at[turn(z, d)])
 
@@ -136,18 +166,25 @@
         arrive(pt.at[s, other_rows], t_s.at[1, s])
         own_table[s].wait()
     nt = (((1,), (1,)), ((), ()))
-    for s in (xh, far):
-        for d in (1, 2, 3):
-            arrive(qb.at[s, rows(turn(z, d))], q_r.at[s, turn(z, d)])
-            for l in (xl, yon):
-                arrive(pt.at[s, half(l, turn(y, d))], p_r.at[s, l, turn(y, d)])
-        for i in range(COLS // R):
-            term = lax.dot_general(pt[s, i * R:(i + 1) * R], qb[s], nt, preferred_element_type=F32)
-            if s is xh:
-                s_own[i * R:(i + 1) * R] = term
-            else:
-                s_own[i * R:(i + 1) * R] += term
-                send(s_own.at[pl.ds(i * R, R)], s_far.at[pl.ds(i * R, R)], c_s.at[i], c_r.at[i], sibling)
+
+    def logits_part(s, i):
+        return lax.dot_general(pt[s, i * R:(i + 1) * R], qb[s], nt, preferred_element_type=F32)
+
+    finish(functools.partial(queries, xh), q_r.at[xh])
+    for l in (xl, yon):
+        finish(functools.partial(passages, xh, l), p_r.at[xh, l])
+    for i in range(2):
+        s_own[i * R:(i + 1) * R] = logits_part(xh, i)
+    on_z(relay, far)
+    on_y(relay, far, xl)
+    for i in range(2, COLS // R):
+        s_own[i * R:(i + 1) * R] = logits_part(xh, i)
+    finish(functools.partial(queries, far), q_r.at[far])
+    for l in (yon, xl):
+        finish(functools.partial(passages, far, l), p_r.at[far, l])
+    for i in range(COLS // R):
+        s_own[i * R:(i + 1) * R] += logits_part(far, i)
+        send(s_own.at[pl.ds(i * R, R)], s_far.at[pl.ds(i * R, R)], c_s.at[i], c_r.at[i], sibling)
     top = jnp.full((1, NB * R), -jnp.inf, F32)
     hit = jnp.zeros((1, NB * R), F32)
     positive = idx[7:8, :]
@@ -210,19 +247,55 @@
     def query_part(s, zz):
         return lax.dot_general(grad[:, rows(zz)], pt[s], tn, preferred_element_type=F32)
 
-    def query_sends(step, s):
-        for d in (1, 2, 3):
-            zz = turn(z, d)
-            qg_part[step, d] = query_part(s, zz).astype(BF16)
-            send(qg_part.at[step, d], rq.at[step, 4 - d], qg_s.at[step, d], qg_r.at[step, 4 - d], device(x, y, zz, k))
-
-    def passage_sends(n, s, l):
-        part = lax.dot_general(grad[rows(l, 4 * H)], qb[s], nn, preferred_element_type=F32)
-        pg_part[n] = part.astype(BF16)
-        px[n] = part
-        for d in (1, 2, 3):
-            yy = turn(y, d)
-            send(pg_part.at[n, rows(yy, H)], rp.at[n, 4 - d], pg_s.at[n, d], pg_r.at[n, 4 - d], device(x, yy, z, k))
+    def query_ahead(n, s):
+        qg_part[n] = query_part(s, turn(z, 2)).astype(BF16)
+        send(qg_part.at[n, pl.ds(0, H)], rqa.at[n, 0], qg_s.at[n, 0], qg_r.at[n, 0], z_next)
+        send(qg_part.at[n, pl.ds(H, H)], rqa.at[n, 1], qg_s.at[n, 1], qg_r.at[n, 1], z_last)
+
+    def query_next(n, s):
+        for way, (d, to) in enumerate(((1, z_next), (3, z_last))):
+            part = query_part(s, turn(z, d))
+            arrive(rqa.at[n, way], qg_r.at[n, way])
+            a, o = way * H, (1 - way) * H
+            qg_on[n, way, a:a + H] = (part[a:a + H] + rqa[n, way].astype(F32)).astype(BF16)
+            qg_on[n, way, o:o + H] = part[o:o + H].astype(BF16)
+            send(qg_on.at[n, way], rq.at[n, way], qg_s.at[n, 2 + way], qg_r.at[n, 2 + way], to)
+
+    def query_sum(n, total):
+        for way in range(2):
+            arrive(rq.at[n, way], qg_r.at[n, 2 + way])
+            total += rq[n, way].astype(F32)
+        return total
+
+    Q = H // 2
+
+    def passage_ahead(n):
+        s, l = order[n]
+        px[n] = lax.dot_general(grad[rows(l, 4 * H)], qb[s], nn, preferred_element_type=F32)
+        pg_part[n] = px[n, rows(turn(y, 2), H)].astype(BF16)
+        send(pg_part.at[n, pl.ds(0, Q)], rpa.at[n, 0], pg_s.at[n, 0], pg_r.at[n, 0], y_next)
+        send(pg_part.at[n, pl.ds(Q, Q)], rpa.at[n, 1], pg_s.at[n, 1], pg_r.at[n, 1], y_last)
+
+    def passage_next(n):
+        for way, (d, to) in enumerate(((1, y_next), (3, y_last))):
+            part = px[n, rows(turn(y, d), H)]
+            arrive(rpa.at[n, way], pg_r.at[n, way])
+            a, o = way * Q, (1 - way) * Q
+            pg_on[n, way, a:a + Q] = (part[a:a + Q] + rpa[n, way].astype(F32)).astype(BF16)
+            pg_on[n, way, o:o + Q] = part[o:o + Q].astype(BF16)
+            send(pg_on.at[n, way], rp.at[n, way], pg_s.at[n, 2 + way], pg_r.at[n, 2 + way], to)
+
+    def passage_sum(n):
+        total = px[n, rows(y, H)]
+        for way in range(2):
+            arrive(rp.at[n, way], pg_r.at[n, 2 + way])
+            total += rp[n, way].astype(F32)
+        return total
+
+    def passage_on(n):
+        s, l = order[n]
+        pg_sum[n] = passage_sum(n).astype(BF16)
+        send(pg_sum.at[n], rpx.at[xh, xl], sx_s.at[n], sx_r.at[xh, xl], device(2 * s + l, y, z, k))
 
     def table_half(l):
         return lax.dot_general(grad[NB * R:], qb[l], nn, preferred_element_type=F32)
@@ -230,15 +303,16 @@
     order = ((far, xl), (far, yon), (xh, yon), (xh, xl))
     tg_part[0] = table_half(yon).astype(BF16)
     send(tg_part.at[0], rtx, tx_s.at[0], tx_s.at[1], device(2 * xh + yon, y, z, k))
-    passage_sends(0, *order[0])
-    query_sends(0, far)
-    passage_sends(1, *order[1])
-    passage_sends(2, *order[2])
-    query_sends(1, xh)
-    passage_sends(3, *order[3])
+    passage_ahead(0)
+    query_ahead(0, far)
+    passage_ahead(1)
+    passage_ahead(2)
+    query_ahead(1, xh)
+    passage_ahead(3)
     tx[...] = table_half(xl)
-    qx[...] = query_part(far, z)
-    qg_out[...] = query_part(xh, z)
+    passage_next(0)
+    query_next(0, far)
+    passage_next(1)
 
     arrive(rtx, tx_s.at[1])
     tx[...] += rtx[...].astype(F32)
@@ -247,27 +321,15 @@
         yy = turn(y, d)
         send(tg_part.at[1, :, rows(yy, CW)], rt.at[4 - d], tg_s.at[d], tg_r.at[4 - d], device(x, yy, z, k))
 
-    def passage_sum(n):
-        total = px[n, rows(y, H)]
-        for d in (1, 2, 3):
-            arrive(rp.at[n, d], pg_r.at[n, d])
-            total += rp[n, d].astype(F32)
-        return total
-
-    def passage_on(n):
-        s, l = order[n]
-        rp[n, 0] = passage_sum(n).astype(BF16)
-        send(rp.at[n, 0], rpx.at[xh, xl], sx_s.at[n], sx_r.at[xh, xl], device(2 * s + l, y, z, k))
-
+    query_next(1, xh)
+    passage_next(2)
+    passage_next(3)
+    qx[...] = query_part(far, z)
     passage_on(0)
-    total = qx[...]
-    for d in (1, 2, 3):
-        arrive(rq.at[0, d], qg_r.at[0, d])
-        total += rq[0, d].astype(F32)
-    rq[0, 0] = total.astype(BF16)
-    send(rq.at[0, 0], rqx, qx_s.at[0], qx_s.at[1], device(opposite, y, z, k))
+    qg_sum[...] = query_sum(0, qx[...]).astype(BF16)
+    send(qg_sum, rqx, qx_s.at[0], qx_s.at[1], device(opposite, y, z, k))
     passage_on(1)
-    passage_on(2)
+    qg_out[...] = query_part(xh, z)
 
     total = tx[:, rows(y, CW)]
     for d in (1, 2, 3):
@@ -289,10 +351,8 @@
                 send(tsum.at[core, h], tt.at[z], tt_s.at[core, h], tt_r.at[z], device(x, dst_y, dst_z, core))
                 sends.pop()
 
-    total = qg_out[...]
-    for d in (1, 2, 3):
-        arrive(rq.at[1, d], qg_r.at[1, d])
-        total += rq[1, d].astype(F32)
+    passage_on(2)
+    total = query_sum(1, qg_out[...])
     arrive(rqx, qx_s.at[1])
     qg_out[...] = total + rqx[...].astype(F32)
     total = passage_sum(3)
@@ -358,12 +418,18 @@
             pltpu.VMEM((COLS, NB * R), F32),
             pltpu.VMEM((COLS, NB * R), BF16),
             pltpu.VMEM((8, 8, NB * R), F32),
-            pltpu.VMEM((2, 4, R, W), BF16),
-            pltpu.VMEM((4, 4 * H, W), BF16),
+            pltpu.VMEM((2, R, W), BF16),
+            pltpu.VMEM((4, H, W), BF16),
             pltpu.VMEM((2, 2 * TR, W), BF16),
-            pltpu.VMEM((2, 4, R, W), BF16),
+            pltpu.VMEM((2, 2, R, W), BF16),
+            pltpu.VMEM((4, 2, H, W), BF16),
+            pltpu.VMEM((2, 2, H, W), BF16),
+            pltpu.VMEM((4, 2, H // 2, W), BF16),
             pltpu.VMEM((R, W), BF16),
-            pltpu.VMEM((4, 4, H, W), BF16),
+            pltpu.VMEM((3, H, W), BF16),
+            pltpu.VMEM((2, 2, R, W), BF16),
+            pltpu.VMEM((R, W), BF16),
+            pltpu.VMEM((4, 2, H, W), BF16),
             pltpu.VMEM((2, 2, H, W), BF16),
             pltpu.VMEM((4, 2 * TR, CW), BF16),
             pltpu.VMEM((2 * TR, W), BF16),
@@ -380,13 +446,13 @@
             pltpu.VMEM((1, NB * R), F32),
             dma((8,)),
             dma((2, 4)), dma((2, 4)),
-            dma((3,)), dma((4, 4)), dma((2, 2, 4)),
+            dma((3,)), dma((2, 2)), dma((2, 2, 4)), dma((2, 2, 4)),
             dma((2, 2)),
             dma((4,)), dma((4,)),
             dma((5,)), dma((5,)),
             dma((8,)), dma((8,)),
             dma((2, 4)), dma((2, 4)),
-            dma((2,)),
+            dma((4,)),
             dma((4, 4)), dma((4, 4)),
             dma((3,)), dma((2, 2)),
             dma((2,)), dma((4,)), dma((4,)),

time: 80.3 us -> 69.9 us (0.87)
  Pallas kernels: 78.1 us -> 68.4 us
    pallas_call x1, Pallas kernels: 76.6 us -> 66.8 us  [per_device(): pl.pallas_call(functools.partial(kernel, factor), name='contrastive', out...]
where the time goes in v3:
time: 69.9 us; the launch traced here: 69 us
  Pallas kernels  68.4 us (98%)
    pallas_call x1, Pallas kernels, per_device(): pl.pallas_call(functools.partial(kernel, factor), name='contrastive', out...  66.8 us
    pallas_call x1, Pallas kernels, per_device(): pl.pallas_call(place, name='place', out_shape=(jax.ShapeDtypeStruct((1, 3...  1.54 us

profile of v3, /device:TPU:0, one launch (start us, length us, event | category | flops | bytes accessed | tf_op | source)
XLA Modules:
  0.0 69.0 jit_solution(4491928592294605082)
XLA Ops:
  0.6 66.8 %contrastive.1 = (f32[8,128]{1,0:T(8,128)S(1)}, f32[128,1024]{1,0:T(8,128)S(1)}, f32[128,1024]{1,0:T(8,128)S(1)}, f32[256,128]{1,0:T(8,128)S(1)}) custom-call(bf16[128,1024]{1,0:T(8,128)(2,1)} %q_in.1, bf16[128,1024]{1,0:T(8,128)(2,1)} %p_in.1, bf16[256,4096]{1,0:T(8,128)(2,1)} %t_in.1, s32[7,128]{1,0:T(8,128)} %bitcast.5, s32[7,128]{1,0:T(8,128)} %bitcast.6, ...), custom_call_target="tpu_custom_call" | custom-call | tf_op jit(solution)/shard_map/contrastive/pallas_call | solution.py:401
  67.5 1.5 %place.1 = (f32[1,32]{1,0:T(1,128)}, f32[128,1024]{1,0:T(8,128)}, f32[128,1024]{1,0:T(8,128)}, f32[256,128]{1,0:T(8,128)}) custom-call(f32[8,128]{1,0:T(8,128)S(1)} %get-tuple-element.12.loss_in, f32[128,1024]{1,0:T(8,128)S(1)} %get-tuple-element.13.qg_in, f32[128,1024]{1,0:T(8,128)S(1)} %get-tuple-element.14.pg_in, f32[256,128]{1,0:T(8,128)S(1)} %get-tuple-element.15.tg_in), custom_call_target="tpu_custom_call" | custom-call | tf_op jit(solution)/shard_map/place/pallas_call | solution.py:468

commit v4 on v3

--- a/solution.py
+++ b/solution.py
@@ -26,9 +26,9 @@
 
 def kernel(
     factor, q_in, p_in, t_in, owner_in, row_in, pos_in, weight_in, loss_out, qg_out, pg_out, tg_out,
-    qb, pt, idx, s_own, s_far, e_buf, grad, stats, qg_part, pg_part, tg_part,
-    qg_on, pg_on, rqa, rpa, qg_sum, pg_sum, rq, rqx, rp, rpx, rt, rtx, tt, qx, px, tx, tsum, p_buf, owner_buf, row_buf, pos_buf, weight_buf, loss_row,
-    in_s, q_s, q_r, px_s, px_r, p_s, p_r, t_s, i_s, i_r, c_s, c_r, st_s, st_r,
+    qb, pt, idx, s_own, s_far, e_buf, grad, stats, hits, counts, qg_part, pg_part, tg_part,
+    qg_on, pg_on, rqa, rpa, qg_sum, pg_sum, rq, rqx, rp, rpx, rt, rtx, tt, qx, px, tx, tsum, p_buf, owner_buf, row_buf, pos_buf, weight_buf, sums,
+    in_s, q_s, q_r, qf_s, qf_r, px_s, px_r, p_s, p_r, t_s, i_s, i_r, c_s, c_r, st_s, st_r,
     qg_s, qg_r, qx_s, pg_s, pg_r, sx_s, sx_r, tx_s, tg_s, tg_r, tt_s, tt_r,
 ):
     b, c = lax.axis_index("blk"), lax.axis_index("corpus")
@@ -100,8 +100,9 @@
     def passages(s, l, d, part=None):
         return pt.at[s, half(l, turn(y, d)) if part is None else rows((l * 4 + turn(y, d)) * 2 + part, H // 2)]
 
-    def queries(s, d, part=None):
-        return qb.at[s, rows(turn(z, d)) if part is None else rows(turn(z, d) * 2 + part, R // 2)]
+    def queries(s, c, d, part=None):
+        n = turn(z, d) * 2 + c
+        return qb.at[s, rows(n, H) if part is None else rows(n * 2 + part, H // 2)]
 
     def spread(block, ss, rs, forward, back):
         send(block(0), block(0), ss.at[1], rs.at[1], forward)
@@ -123,34 +124,27 @@
     def on_y(step, s, l):
         step(functools.partial(passages, s, l), p_s.at[s, l], p_r.at[s, l], y_next, y_last)
 
-    def on_z(step, s):
-        step(functools.partial(queries, s), q_s.at[s], q_r.at[s], z_next, z_last)
-
-    def first_sends():
-        mine = pt.at[xh, half(xl, y)]
-        send(p_buf.at[rows(xh, H)], mine, px_s.at[0], px_r.at[xh, xl], device(2 * xh + yon, y, z, k))
-        send(p_buf.at[rows(far, H)], mine, px_s.at[1], px_r.at[xh, xl], device(2 * far + yon, y, z, k))
-        on_y(spread, xh, xl)
-        on_z(spread, xh)
-        send(queries(xh, 0), queries(xh, 0), qx_s.at[2], qx_s.at[3], device(opposite, y, z, k))
-        send(p_buf.at[rows(far, H)], mine, px_s.at[2], px_r.at[xh, xl], device(opposite, y, z, k))
-
-    first_sends()
+    def on_z(step, s, c):
+        step(functools.partial(queries, s, c), q_s.at[s, c], q_r.at[s, c], z_next, z_last)
+
     for d in (1, 2, 3):
         send(idx.at[:, rows(z)], idx.at[:, rows(z)], i_s.at[d], i_r.at[z], device(x, y, turn(z, d), k))
+    mine = pt.at[xh, half(xl, y)]
+    send(p_buf.at[rows(xh, H)], mine, px_s.at[0], px_r.at[xh, xl], device(2 * xh + yon, y, z, k))
+    send(p_buf.at[rows(far, H)], mine, px_s.at[1], px_r.at[xh, xl], device(2 * far + yon, y, z, k))
+    on_y(spread, xh, xl)
+    for n in range(2):
+        on_z(spread, xh, n)
+    for n in range(2):
+        send(queries(xh, n, 0), queries(xh, n, 0), qf_s.at[n], qf_r.at[n], device(opposite, y, z, k))
+    send(p_buf.at[rows(far, H)], mine, px_s.at[2], px_r.at[xh, xl], device(opposite, y, z, k))
     for s in range(2):
         send(table_part(s, 1 - k), pt.at[s, table_rows], t_s.at[0, s], t_s.at[1, s], sibling)
     for s in (xh, far):
         arrive(passages(s, yon, 0), px_r.at[s, yon])
         on_y(spread, s, yon)
     on_y(relay, xh, xl)
-    on_z(relay, xh)
-    on_y(relay, xh, yon)
-    arrive(queries(far, 0), qx_s.at[3])
-    on_z(spread, far)
-    on_y(relay, far, yon)
-    arrive(passages(far, xl, 0), px_r.at[far, xl])
-    on_y(spread, far, xl)
+    on_z(relay, xh, 0)
     for d in (1, 2, 3):
         arrive(idx.at[:, rows(turn(z, d))], i_r.at[turn(z, d)])
 
@@ -160,6 +154,16 @@
     count = jnp.zeros((2 * TR, NB * R), F32)
     for n in range(7):
         count += (idx[n:n + 1, :] == named).astype(F32)
+    counts[...] = count
+    on_z(relay, xh, 1)
+    arrive(queries(far, 0, 0), qf_r.at[0])
+    on_z(spread, far, 0)
+    on_y(relay, xh, yon)
+    arrive(queries(far, 1, 0), qf_r.at[1])
+    on_z(spread, far, 1)
+    on_y(relay, far, yon)
+    arrive(passages(far, xl, 0), px_r.at[far, xl])
+    on_y(spread, far, xl)
 
     other_rows = pl.ds(NB * R + pl.multiple_of((1 - k) * TR, TR), TR)
     for s in range(2):
@@ -170,22 +174,24 @@
     def logits_part(s, i):
         return lax.dot_general(pt[s, i * R:(i + 1) * R], qb[s], nt, preferred_element_type=F32)
 
-    finish(functools.partial(queries, xh), q_r.at[xh])
+    for n in range(2):
+        finish(functools.partial(queries, xh, n), q_r.at[xh, n])
     for l in (xl, yon):
         finish(functools.partial(passages, xh, l), p_r.at[xh, l])
     for i in range(2):
         s_own[i * R:(i + 1) * R] = logits_part(xh, i)
-    on_z(relay, far)
+    on_z(relay, far, 0)
     on_y(relay, far, xl)
+    on_z(relay, far, 1)
     for i in range(2, COLS // R):
         s_own[i * R:(i + 1) * R] = logits_part(xh, i)
-    finish(functools.partial(queries, far), q_r.at[far])
+    for n in range(2):
+        finish(functools.partial(queries, far, n), q_r.at[far, n])
     for l in (yon, xl):
         finish(functools.partial(passages, far, l), p_r.at[far, l])
     for i in range(COLS // R):
         s_own[i * R:(i + 1) * R] += logits_part(far, i)
         send(s_own.at[pl.ds(i * R, R)], s_far.at[pl.ds(i * R, R)], c_s.at[i], c_r.at[i], sibling)
-    top = jnp.full((1, NB * R), -jnp.inf, F32)
     hit = jnp.zeros((1, NB * R), F32)
     positive = idx[7:8, :]
 
@@ -194,50 +200,50 @@
         r = r + jnp.where(r >= H, 4 * R - H, 0) + (i // 2 * 2048 + i % 2 * 1024) + z * R + xh * H
         return r.astype(F32) == positive
 
+    tops, masses = [], []
+    count = counts[...]
     for i in range(COLS // R):
         arrive(s_far.at[pl.ds(i * R, R)], c_r.at[i])
         total = (s_own[i * R:(i + 1) * R] + s_far[i * R:(i + 1) * R]) * factor
-        e_buf[i * R:(i + 1) * R] = total
         if i < NB:
             hit += jnp.sum(jnp.where(here(i), total, 0.0), axis=0, keepdims=True)
+            top = jnp.max(total, axis=0, keepdims=True)
+            e = jnp.exp(total - top)
         else:
-            total = jnp.where(count > 0, total, -jnp.inf)
-        top = jnp.maximum(top, jnp.max(total, axis=0, keepdims=True))
-    mass = jnp.zeros((1, NB * R), F32)
-    for i in range(COLS // R):
-        if i < NB:
-            e = jnp.exp(e_buf[i * R:(i + 1) * R] - top)
-        else:
-            e = count * jnp.exp(jnp.where(count > 0, e_buf[i * R:(i + 1) * R] - top, 0.0))
+            top = jnp.max(jnp.where(count > 0, total, -jnp.inf), axis=0, keepdims=True)
+            e = count * jnp.exp(jnp.where(count > 0, total - top, 0.0))
         e_buf[i * R:(i + 1) * R] = e
-        mass += jnp.sum(e, axis=0, keepdims=True)
+        tops.append(top)
+        masses.append(jnp.sum(e, axis=0, keepdims=True))
+    top = functools.reduce(jnp.maximum, tops)
+    mass = sum(m * jnp.exp(t - top) for m, t in zip(masses, tops))
     me = xh * 4 + z
-    stats[me, 0:1] = top
-    stats[me, 1:2] = mass
-    stats[me, 2:3] = hit
-    for n in range(1, 8):
+    for n in range(NB):
+        stats[me, n:n + 1] = top[:, n * R:(n + 1) * R]
+        stats[me, NB + n:NB + n + 1] = mass[:, n * R:(n + 1) * R]
+        hits[me, n:n + 1] = hit[:, n * R:(n + 1) * R]
+    there = []
+    for n in range(7, 0, -1):
         dx, d = n // 4, n % 4
-        send(stats.at[me], stats.at[me], st_s.at[n], st_r.at[me], device(turn(x, 2 * dx), y, turn(z, d), k))
+        there.append(device(turn(x, 2 * dx), y, turn(z, d), k))
+        send(stats.at[me], stats.at[me], st_s.at[0, n], st_r.at[0, me], there[-1])
+    for n in range(7, 0, -1):
+        send(hits.at[me], hits.at[me], st_s.at[1, n], st_r.at[1, me], there[7 - n])
     for n in range(1, 8):
         dx, d = n // 4, n % 4
         slot = lax.rem(xh + dx, 2) * 4 + turn(z, d)
-        arrive(stats.at[slot], st_r.at[slot])
-    row_top = stats[0, 0:1]
+        arrive(stats.at[slot], st_r.at[0, slot])
+    row_top = stats[0, 0:NB]
     for n in range(1, 8):
-        row_top = jnp.maximum(row_top, stats[n, 0:1])
-    mass = jnp.zeros((1, NB * R), F32)
-    hit = jnp.zeros((1, NB * R), F32)
+        row_top = jnp.maximum(row_top, stats[n, 0:NB])
+    mass = jnp.zeros((NB, R), F32)
     for n in range(8):
-        mass += stats[n, 1:2] * jnp.exp(stats[n, 0:1] - row_top)
-        hit += stats[n, 2:3]
-    log_total = row_top + jnp.log(mass)
-    loss_row[...] = log_total - hit
-    own_loss = jnp.broadcast_to(loss_row[:, rows(z)], (8, R))
-    loss_out[...] = pltpu.roll(own_loss, lax.rem(R - c * 32, R), 1)
+        mass += stats[n, NB:2 * NB] * jnp.exp(stats[n, 0:NB] - row_top)
+    sums[...] = row_top + jnp.log(mass)
+    log_total = jnp.concatenate([sums[n:n + 1] for n in range(NB)], axis=1)
     weight = idx[8:9, :] * factor
-    scale = weight * jnp.exp(top - log_total)
     for i in range(COLS // R):
-        g = scale * e_buf[i * R:(i + 1) * R]
+        g = weight * jnp.exp(tops[i] - log_total) * e_buf[i * R:(i + 1) * R]
         if i < NB:
             g = g - jnp.where(here(i), weight, 0.0)
         grad[i * R:(i + 1) * R] = g.astype(BF16)
@@ -301,10 +307,10 @@
         return lax.dot_general(grad[NB * R:], qb[l], nn, preferred_element_type=F32)
 
     order = ((far, xl), (far, yon), (xh, yon), (xh, xl))
+    passage_ahead(0)
+    query_ahead(0, far)
     tg_part[0] = table_half(yon).astype(BF16)
     send(tg_part.at[0], rtx, tx_s.at[0], tx_s.at[1], device(2 * xh + yon, y, z, k))
-    passage_ahead(0)
-    query_ahead(0, far)
     passage_ahead(1)
     passage_ahead(2)
     query_ahead(1, xh)
@@ -313,6 +319,7 @@
     passage_next(0)
     query_next(0, far)
     passage_next(1)
+    passage_next(2)
 
     arrive(rtx, tx_s.at[1])
     tx[...] += rtx[...].astype(F32)
@@ -322,7 +329,6 @@
         send(tg_part.at[1, :, rows(yy, CW)], rt.at[4 - d], tg_s.at[d], tg_r.at[4 - d], device(x, yy, z, k))
 
     query_next(1, xh)
-    passage_next(2)
     passage_next(3)
     qx[...] = query_part(far, z)
     passage_on(0)
@@ -369,6 +375,17 @@
             arrive(tt.at[zz], tt_r.at[zz])
 
         tg_out[zz * TR:(zz + 1) * TR] = tt[zz]
+
+    for n in range(1, 8):
+        dx, d = n // 4, n % 4
+        slot = lax.rem(xh + dx, 2) * 4 + turn(z, d)
+        arrive(hits.at[slot], st_r.at[1, slot])
+    hit = jnp.zeros((NB, R), F32)
+    for n in range(8):
+        hit += hits[n, 0:NB]
+    own_block = lax.broadcasted_iota(jnp.int32, (NB, R), 0) == z
+    own_loss = jnp.sum(jnp.where(own_block, sums[...] - hit, 0.0), axis=0, keepdims=True)
+    loss_out[...] = pltpu.roll(jnp.broadcast_to(own_loss, (8, R)), lax.rem(R - c * 32, R), 1)
 
     for copy in sends:
         copy.wait_send()
@@ -417,7 +434,9 @@
             pltpu.VMEM((COLS, NB * R), F32),
             pltpu.VMEM((COLS, NB * R), F32),
             pltpu.VMEM((COLS, NB * R), BF16),
-            pltpu.VMEM((8, 8, NB * R), F32),
+            pltpu.VMEM((8, 2 * NB, R), F32),
+            pltpu.VMEM((8, 2 * NB, R), F32),
+            pltpu.VMEM((2 * TR, NB * R), F32),
             pltpu.VMEM((2, R, W), BF16),
             pltpu.VMEM((4, H, W), BF16),
             pltpu.VMEM((2, 2 * TR, W), BF16),
@@ -443,16 +462,16 @@
             pltpu.VMEM((7, R), jnp.int32),
             pltpu.VMEM((1, R), jnp.int32),
             pltpu.VMEM((1, R), F32),
-            pltpu.VMEM((1, NB * R), F32),
+            pltpu.VMEM((NB, R), F32),
             dma((8,)),
-            dma((2, 4)), dma((2, 4)),
+            dma((2, 2, 4)), dma((2, 2, 4)), dma((2,)), dma((2,)),
             dma((3,)), dma((2, 2)), dma((2, 2, 4)), dma((2, 2, 4)),
             dma((2, 2)),
             dma((4,)), dma((4,)),
             dma((5,)), dma((5,)),
-            dma((8,)), dma((8,)),
+            dma((2, 8)), dma((2, 8)),
             dma((2, 4)), dma((2, 4)),
-            dma((4,)),
+            dma((2,)),
             dma((4, 4)), dma((4, 4)),
             dma((3,)), dma((2, 2)),
             dma((2,)), dma((4,)), dma((4,)),

time: 69.9 us -> 68.2 us (0.976)
  Pallas kernels: 68.4 us -> 66.5 us
    pallas_call x1, Pallas kernels: 66.8 us -> 64.9 us  [per_device(): pl.pallas_call(functools.partial(kernel, factor), name='contrastive', out...]
where the time goes in v4:
time: 68.2 us; the launch traced here: 67.1 us
  Pallas kernels  66.5 us (98%)
    pallas_call x1, Pallas kernels, per_device(): pl.pallas_call(functools.partial(kernel, factor), name='contrastive', out...  64.9 us
    pallas_call x1, Pallas kernels, per_device(): pl.pallas_call(place, name='place', out_shape=(jax.ShapeDtypeStruct((1, 3...  1.54 us

profile of v4, /device:TPU:0, one launch (start us, length us, event | category | flops | bytes accessed | tf_op | source)
XLA Modules:
  0.0 67.1 jit_solution(1971546046452828193)
XLA Ops:
  0.6 64.9 %contrastive.1 = (f32[8,128]{1,0:T(8,128)S(1)}, f32[128,1024]{1,0:T(8,128)S(1)}, f32[128,1024]{1,0:T(8,128)S(1)}, f32[256,128]{1,0:T(8,128)S(1)}) custom-call(bf16[128,1024]{1,0:T(8,128)(2,1)} %q_in.1, bf16[128,1024]{1,0:T(8,128)(2,1)} %p_in.1, bf16[256,4096]{1,0:T(8,128)(2,1)} %t_in.1, s32[7,128]{1,0:T(8,128)} %bitcast.5, s32[7,128]{1,0:T(8,128)} %bitcast.6, ...), custom_call_target="tpu_custom_call" | custom-call | tf_op jit(solution)/shard_map/contrastive/pallas_call | solution.py:418
  65.6 1.5 %place.1 = (f32[1,32]{1,0:T(1,128)}, f32[128,1024]{1,0:T(8,128)}, f32[128,1024]{1,0:T(8,128)}, f32[256,128]{1,0:T(8,128)}) custom-call(f32[8,128]{1,0:T(8,128)S(1)} %get-tuple-element.12.loss_in, f32[128,1024]{1,0:T(8,128)S(1)} %get-tuple-element.13.qg_in, f32[128,1024]{1,0:T(8,128)S(1)} %get-tuple-element.14.pg_in, f32[256,128]{1,0:T(8,128)S(1)} %get-tuple-element.15.tg_in), custom_call_target="tpu_custom_call" | custom-call | tf_op jit(solution)/shard_map/place/pallas_call | solution.py:487

commit v5 on v4

--- a/solution.py
+++ b/solution.py
@@ -27,9 +27,9 @@
 def kernel(
     factor, q_in, p_in, t_in, owner_in, row_in, pos_in, weight_in, loss_out, qg_out, pg_out, tg_out,
     qb, pt, idx, s_own, s_far, e_buf, grad, stats, hits, counts, qg_part, pg_part, tg_part,
-    qg_on, pg_on, rqa, rpa, qg_sum, pg_sum, rq, rqx, rp, rpx, rt, rtx, tt, qx, px, tx, tsum, p_buf, owner_buf, row_buf, pos_buf, weight_buf, sums,
+    qg_on, pg_on, rqa, rpa, qg_sum, pg_sum, rq, rqx, rp, rpx, rt, rtx, tt, qx, qn, px, tx, tsum, p_buf, owner_buf, row_buf, pos_buf, weight_buf, sums,
     in_s, q_s, q_r, qf_s, qf_r, px_s, px_r, p_s, p_r, t_s, i_s, i_r, c_s, c_r, st_s, st_r,
-    qg_s, qg_r, qx_s, pg_s, pg_r, sx_s, sx_r, tx_s, tg_s, tg_r, tt_s, tt_r,
+    qg_s, qg_r, qx_s, qx_r, pg_s, pg_r, sx_s, sx_r, tx_s, tg_s, tg_r, tt_s, tt_r,
 ):
     b, c = lax.axis_index("blk"), lax.axis_index("corpus")
     xl, y, z = lax.div(b, 16), lax.rem(lax.div(b, 4), 4), lax.rem(b, 4)
@@ -259,19 +259,30 @@
         send(qg_part.at[n, pl.ds(H, H)], rqa.at[n, 1], qg_s.at[n, 1], qg_r.at[n, 1], z_last)
 
     def query_next(n, s):
-        for way, (d, to) in enumerate(((1, z_next), (3, z_last))):
-            part = query_part(s, turn(z, d))
-            arrive(rqa.at[n, way], qg_r.at[n, way])
-            a, o = way * H, (1 - way) * H
-            qg_on[n, way, a:a + H] = (part[a:a + H] + rqa[n, way].astype(F32)).astype(BF16)
-            qg_on[n, way, o:o + H] = part[o:o + H].astype(BF16)
-            send(qg_on.at[n, way], rq.at[n, way], qg_s.at[n, 2 + way], qg_r.at[n, 2 + way], to)
-
-    def query_sum(n, total):
+        ways = ((1, z_next), (3, z_last))
+        for way, (d, to) in enumerate(ways):
+            qn[way] = query_part(s, turn(z, d))
+        for chunk in range(2):
+            at = pl.ds(chunk * H, H)
+            for way, (d, to) in enumerate(ways):
+                part = qn[way, chunk * H:(chunk + 1) * H]
+                if chunk == way:
+                    arrive(rqa.at[n, way], qg_r.at[n, way])
+                    part += rqa[n, way].astype(F32)
+                qg_on[n, way, chunk * H:(chunk + 1) * H] = part.astype(BF16)
+                sem = 2 + chunk * 2 + way
+                send(qg_on.at[n, way, at], rq.at[n, way, at], qg_s.at[n, sem], qg_r.at[n, sem], to)
+
+    def query_sum(n, chunk, total):
         for way in range(2):
-            arrive(rq.at[n, way], qg_r.at[n, 2 + way])
-            total += rq[n, way].astype(F32)
+            arrive(rq.at[n, way, pl.ds(chunk * H, H)], qg_r.at[n, 2 + chunk * 2 + way])
+            total += rq[n, way, chunk * H:(chunk + 1) * H].astype(F32)
         return total
+
+    def query_on(chunk):
+        at = pl.ds(chunk * H, H)
+        qg_sum[chunk * H:(chunk + 1) * H] = query_sum(0, chunk, qx[chunk * H:(chunk + 1) * H]).astype(BF16)
+        send(qg_sum.at[at], rqx.at[at], qx_s.at[chunk], qx_r.at[chunk], device(opposite, y, z, k))
 
     Q = H // 2
 
@@ -332,10 +343,11 @@
     passage_next(3)
     qx[...] = query_part(far, z)
     passage_on(0)
-    qg_sum[...] = query_sum(0, qx[...]).astype(BF16)
-    send(qg_sum, rqx, qx_s.at[0], qx_s.at[1], device(opposite, y, z, k))
+    query_on(0)
     passage_on(1)
+    query_on(1)
     qg_out[...] = query_part(xh, z)
+    passage_on(2)
 
     total = tx[:, rows(y, CW)]
     for d in (1, 2, 3):
@@ -357,10 +369,11 @@
                 send(tsum.at[core, h], tt.at[z], tt_s.at[core, h], tt_r.at[z], device(x, dst_y, dst_z, core))
                 sends.pop()
 
-    passage_on(2)
-    total = query_sum(1, qg_out[...])
-    arrive(rqx, qx_s.at[1])
-    qg_out[...] = total + rqx[...].astype(F32)
+    for chunk in range(2):
+        at = slice(chunk * H, (chunk + 1) * H)
+        total = query_sum(1, chunk, qg_out[at])
+        arrive(rqx.at[pl.ds(chunk * H, H)], qx_r.at[chunk])
+        qg_out[at] = total + rqx[at].astype(F32)
     total = passage_sum(3)
     arrive(rpx.at[xh, yon], sx_r.at[xh, yon])
     pg_out[rows(xh, H)] = total + rpx[xh, yon].astype(F32)
@@ -454,6 +467,7 @@
             pltpu.VMEM((2 * TR, W), BF16),
             pltpu.VMEM((4, TR, 128), F32),
             pltpu.VMEM((R, W), F32),
+            pltpu.VMEM((2, R, W), F32),
             pltpu.VMEM((4, 4 * H, W), F32),
             pltpu.VMEM((2 * TR, W), F32),
             pltpu.VMEM((2, 2, TR, 128), F32),
@@ -470,8 +484,8 @@
             dma((4,)), dma((4,)),
             dma((5,)), dma((5,)),
             dma((2, 8)), dma((2, 8)),
-            dma((2, 4)), dma((2, 4)),
-            dma((2,)),
+            dma((2, 6)), dma((2, 6)),
+            dma((2,)), dma((2,)),
             dma((4, 4)), dma((4, 4)),
             dma((3,)), dma((2, 2)),
             dma((2,)), dma((4,)), dma((4,)),

time: 68.2 us -> 68 us (level)
  no operation moved by 1% of the time
where the time goes in v5:
time: 68 us; the launch traced here: 66.9 us
  Pallas kernels  66.3 us (98%)
    pallas_call x1, Pallas kernels, per_device(): pl.pallas_call(functools.partial(kernel, factor), name='contrastive', out...  64.7 us
    pallas_call x1, Pallas kernels, per_device(): pl.pallas_call(place, name='place', out_shape=(jax.ShapeDtypeStruct((1, 3...  1.54 us

profile of v5, /device:TPU:0, one launch (start us, length us, event | category | flops | bytes accessed | tf_op | source)
XLA Modules:
  0.0 66.9 jit_solution(10079164457198194310)
XLA Ops:
  0.6 64.7 %contrastive.1 = (f32[8,128]{1,0:T(8,128)S(1)}, f32[128,1024]{1,0:T(8,128)S(1)}, f32[128,1024]{1,0:T(8,128)S(1)}, f32[256,128]{1,0:T(8,128)S(1)}) custom-call(bf16[128,1024]{1,0:T(8,128)(2,1)} %q_in.1, bf16[128,1024]{1,0:T(8,128)(2,1)} %p_in.1, bf16[256,4096]{1,0:T(8,128)(2,1)} %t_in.1, s32[7,128]{1,0:T(8,128)} %bitcast.5, s32[7,128]{1,0:T(8,128)} %bitcast.6, ...), custom_call_target="tpu_custom_call" | custom-call | tf_op jit(solution)/shard_map/contrastive/pallas_call | solution.py:431
  65.4 1.5 %place.1 = (f32[1,32]{1,0:T(1,128)}, f32[128,1024]{1,0:T(8,128)}, f32[128,1024]{1,0:T(8,128)}, f32[256,128]{1,0:T(8,128)}) custom-call(f32[8,128]{1,0:T(8,128)S(1)} %get-tuple-element.12.loss_in, f32[128,1024]{1,0:T(8,128)S(1)} %get-tuple-element.13.qg_in, f32[128,1024]{1,0:T(8,128)S(1)} %get-tuple-element.14.pg_in, f32[256,128]{1,0:T(8,128)S(1)} %get-tuple-element.15.tg_in), custom_call_target="tpu_custom_call" | custom-call | tf_op jit(solution)/shard_map/place/pallas_call | solution.py:501
